TPU v7x, 32 devices: a whole 2x2x4 slice. The times are simulated.
32 devices in a mesh: tm: 4 (over x, core), space: 8 (over z, y).
Axes of the slice: x: 2, y: 2, z: 4, core: 2. Of those that a mesh axis runs over, the one named last changes fastest.
Arguments:
- enthalpy: float32 [4, 64, 512, 128], P('tm', 'space'), may hold values from -4 to 4
- solute: float32 [4, 64, 512, 128], P('tm', 'space'), may hold values from 0.5 to 1.5
- material: int32 [64, 512, 128], P('space'), may hold values from 0 to 3
- phase_flag: int32 [64, 512, 128], P('space'), may hold values from 0 to 2
- heat_capacity: float32 [4], replicated, may hold values from 0.8 to 2
- latent: float32 [4], replicated, may hold values from 0.5 to 2
- solidus: float32 [4], replicated, may hold values from -0.5 to 0.5
- partition: float32 [4], replicated, may hold values from 0.3 to 0.6
- back_diffusion: float32 [4], replicated, may hold values from 0.1 to 1
- heat_rate: float32 [4], replicated, may hold values from 0.06 to 0.16
- solute_rate: float32 [3], replicated, may hold values from 0.005 to 0.045
Outputs:
- end_enthalpy: float32 [4, 64, 512, 128], P('tm', 'space')
- end_solute: float32 [4, 64, 512, 128], P('tm', 'space')
All inputs are finite; a program needn't handle non-finite values.
Results may differ from a plain program's by a relative error of at most 0.00002.
Values sent between devices are 32-bit elements; how exact they have to be, the bound alone decides.
No kernel may reach another device: no remote copies, remote signals or barrier semaphores. Data moves between devices by JAX's collectives and lax.ppermute only.
A program may use at most 128 MiB of HBM per device.

v0:
```python
import jax
import jax.numpy as jnp
from jax import lax
from jax.sharding import PartitionSpec as P

STEPS = 4


def with_halo(cells, sides, width):
    for axis, dim in sides:
        count = lax.axis_size(axis)
        ends = count - 1
        head = lax.slice_in_dim(cells, 0, width, axis=dim)
        tail = lax.slice_in_dim(cells, cells.shape[dim] - width, cells.shape[dim], axis=dim)
        cells = jnp.concatenate(
            [
                lax.ppermute(tail, axis, [(i, (i + 1) % count) for i in range(ends)]),
                cells,
                lax.ppermute(head, axis, [((i + 1) % count, i) for i in range(ends)]),
            ],
            axis=dim,
        )
    return cells


def shifted(x, axis, by):
    size = lax.axis_size(axis)
    pairs = [(i, i + by) for i in range(size) if 0 <= i + by < size]
    return lax.ppermute(x, axis, pairs)


def lookup(region_ids, table_values):
    summed = jnp.zeros(region_ids.shape, jnp.float32)
    for member in range(table_values.shape[0]):
        summed = summed + jnp.where(
            region_ids == member, table_values[member], jnp.zeros((), jnp.float32)
        )
    return summed


def coefficients(
    material,
    phase_flag,
    heat_capacity,
    latent,
    solidus,
    partition,
    back_diffusion,
    heat_rate,
    solute_rate,
):
    enthalpy_buffer_capacity = lookup(material, heat_capacity)
    melting_energy_map = lookup(material, latent)
    solidus_field = lookup(material, solidus)
    partition_field = lookup(material, partition)
    backflow = lookup(material, back_diffusion)
    thermal_ratio = lookup(material, heat_rate)
    heat_gain = thermal_ratio * enthalpy_buffer_capacity
    solute_gain = lookup(phase_flag, solute_rate)
    rate_pair = jnp.stack([heat_gain, solute_gain])
    coarse_rates = jnp.stack(
        [
            4.0 * heat_gain / (1.0 + 18.0 * thermal_ratio),
            4.0 * solute_gain / (1.0 + 18.0 * solute_gain / partition_field),
        ]
    )
    return (
        (enthalpy_buffer_capacity, melting_energy_map, solidus_field, partition_field, backflow),
        rate_pair,
        coarse_rates,
    )


def fractions(gridded_quantities, coefs):
    enthalpy_buffer_capacity, melting_energy_map, solidus_field, partition_field, backflow = coefs
    molten_share = jnp.clip((gridded_quantities[0] - solidus_field) / melting_energy_map, 0.0, 1.0)
    local_warmth_value = (
        gridded_quantities[0] - melting_energy_map * molten_share
    ) / enthalpy_buffer_capacity
    denominator_quantity = 1.0 - (1.0 - partition_field) * (1.0 - molten_share) / (1.0 + backflow)
    return jnp.stack([local_warmth_value, gridded_quantities[1] / denominator_quantity])


def laplace(padded):
    middle = padded[:, 1:-1]
    sides = jnp.pad(middle, ((0, 0), (0, 0), (1, 1), (1, 1)))
    return (
        padded[:, 2:]
        + padded[:, :-2]
        + sides[:, :, 2:, 1:-1]
        + sides[:, :, :-2, 1:-1]
        + sides[:, :, 1:-1, 2:]
        + sides[:, :, 1:-1, :-2]
        - 6.0 * middle
    )


def per_device(
    enthalpy,
    solute,
    material,
    phase_flag,
    heat_capacity,
    latent,
    solidus,
    partition,
    back_diffusion,
    heat_rate,
    solute_rate,
):
    gridded_quantities = jnp.stack([enthalpy[0], solute[0]])
    initial = gridded_quantities
    first_laplacian = None
    coefs, rate_pair, coarse_rates = coefficients(
        material,
        phase_flag,
        heat_capacity,
        latent,
        solidus,
        partition,
        back_diffusion,
        heat_rate,
        solute_rate,
    )
    for domain_portion in range(STEPS):
        padded = with_halo(fractions(gridded_quantities, coefs), (("space", 1),), 1)
        laplacian = laplace(padded)
        if domain_portion == 0:
            first_laplacian = laplacian
        gridded_quantities = gridded_quantities + rate_pair * laplacian
    coarse = initial + coarse_rates * first_laplacian
    correction = gridded_quantities - coarse
    position = lax.axis_index("tm")
    result = gridded_quantities
    for domain_portion in range(1, lax.axis_size("tm")):
        arrived = shifted(result, "tm", 1)
        padded = with_halo(fractions(arrived, coefs), (("space", 1),), 1)
        predicted = arrived + coarse_rates * laplace(padded)
        result = jnp.where(position == 0, result, predicted + correction)
    return (result[0][None], result[1][None])


def solution(mesh):
    return jax.shard_map(
        per_device,
        mesh=mesh,
        in_specs=(
            P("tm", "space", None, None),
            P("tm", "space", None, None),
            P("space", None, None),
            P("space", None, None),
            P(),
            P(),
            P(),
            P(),
            P(),
            P(),
            P(),
        ),
        out_specs=(P("tm", "space", None, None), P("tm", "space", None, None)),
        check_vma=False,
    )
```

profile of v0, /device:TPU:6, one launch (start us, length us, event | category | flops | bytes accessed | tf_op | source)
XLA Modules:
  0.0 620.9 jit_solution(9298225944617919321)
XLA Ops:
  9.3 9.9 %divide_bitcast_fusion.4 = (f32[1,8,512,128]{3,2,1,0:T(8,128)}, pred[8,512,128]{2,1,0:T(8,128)(4,1)S(1)}, pred[8,512,128]{2,1,0:T(8,128)(4,1)S(1)}, pred[8,512,128]{2,1,0:T(8,128)(4,1)S(1)}, pred[8,512,128]{2,1,0:T(8,128)(4,1)S(1)}) fusion(f32[]{:T(128)} %bitcast.3, f32[]{:T(128)} %bitcast.2, f32[]{:T(128)} %bitcast.1, f32[]{:T(128)} %bitcast, f32[]{:T(128)} %bitcast.7, ...), kind=kLoop, calls=%fused_computation.194 | loop fusion | flops 12058624 | bytes 6291488 | tf_op jit(solution)/shard_map/stack | solution.py:61
  19.3 10.0 %fusion.76 = f32[1,8,512,128]{3,2,1,0:T(8,128)S(1)} fusion(f32[1,8,512,128]{3,2,1,0:T(8,128)S(1)} %copy-done.24, pred[8,512,128]{2,1,0:T(8,128)(4,1)S(1)} %get-tuple-element.6, f32[]{:T(128)} %bitcast.7, pred[8,512,128]{2,1,0:T(8,128)(4,1)S(1)} %get-tuple-element.5, f32[]{:T(128)} %bitcast.6, pred[8,512,128]{2,1,0:T(8,128)(4,1)S(1)} %get-tuple-element.4, ...), kind=kLoop, calls=%fused_computation.186 | loop fusion | flops 14155776 | bytes 6291504 | tf_op jit(solution)/shard_map/stack | solution.py:81
  29.3 13.4 %fusion.72 = f32[1,8,512,128]{3,2,1,0:T(8,128)S(1)} fusion(f32[1,8,512,128]{3,2,1,0:T(8,128)S(1)} %copy-done.25, f32[1,8,512,128]{3,2,1,0:T(8,128)S(1)} %copy-done.24, pred[8,512,128]{2,1,0:T(8,128)(4,1)S(1)} %get-tuple-element.6, f32[]{:T(128)} %bitcast.31, pred[8,512,128]{2,1,0:T(8,128)(4,1)S(1)} %get-tuple-element.5, f32[]{:T(128)} %bitcast.30, ...), kind=kLoop, calls=%fused_computation.180 | loop fusion | flops 19922944 | bytes 8388672 | tf_op jit(solution)/shard_map/stack | solution.py:81
  55.7 7.8 %divide_bitcast_fusion.3 = (f32[1,8,512,128]{3,2,1,0:T(8,128)}, f32[1,8,512,128]{3,2,1,0:T(8,128)S(1)}) fusion(s32[8,512,128]{2,1,0:T(8,128)S(1)} %copy-done.26, f32[]{:T(128)} %bitcast.11, f32[]{:T(128)} %bitcast.10, f32[]{:T(128)} %bitcast.9, pred[8,512,128]{2,1,0:T(8,128)(4,1)S(1)} %get-tuple-element.6, f32[]{:T(128)} %bitcast.27, ...), kind=kLoop, calls=%fused_computation.193 | loop fusion | flops 10485760 | bytes 8388636 | tf_op jit(solution)/shard_map/stack | solution.py:61
  63.5 8.0 %fusion.78 = f32[1,8,512,128]{3,2,1,0:T(8,128)} fusion(pred[8,512,128]{2,1,0:T(8,128)(4,1)S(1)} %get-tuple-element.6, pred[8,512,128]{2,1,0:T(8,128)(4,1)S(1)} %get-tuple-element.5, pred[8,512,128]{2,1,0:T(8,128)(4,1)S(1)} %get-tuple-element.4, pred[8,512,128]{2,1,0:T(8,128)(4,1)S(1)} %get-tuple-element.3, f32[]{:T(128)} %bitcast.3, f32[]{:T(128)} %bitcast.2, ...), kind=kLoop, calls=%fused_computation.209 | loop fusion | flops 7864320 | bytes 4194336 | tf_op jit(solution)/shard_map/stack | solution.py:60
  71.4 15.0 %multiply_add_fusion = (f32[2,8,512,128]{3,2,1,0:T(8,128)}, f32[2,8,512,128]{3,2,1,0:T(8,128)}) fusion(f32[2,8,512,128]{3,2,1,0:T(8,128)S(1)} %constant_dynamic-update-slice_fusion, f32[1,8,512,128]{3,2,1,0:T(8,128)S(1)} %get-tuple-element.26, f32[1,8,512,128]{3,2,1,0:T(8,128)} %fusion.78, f32[2,8,512,128]{3,2,1,0:T(8,128)} %pad_maximum_fusion, ...), kind=kLoop, calls=%fused_computation.154 | loop fusion | flops 14680064 | bytes 26214400 | tf_op jit(solution)/shard_map/add | solution.py:130
  86.5 15.2 %fusion.71 = f32[1,8,512,128]{3,2,1,0:T(8,128)S(1)} fusion(f32[2,8,512,128]{3,2,1,0:T(8,128)} %get-tuple-element.7, pred[8,512,128]{2,1,0:T(8,128)(4,1)S(1)} %get-tuple-element.6, f32[]{:T(128)} %bitcast.31, pred[8,512,128]{2,1,0:T(8,128)(4,1)S(1)} %get-tuple-element.5, f32[]{:T(128)} %bitcast.30, pred[8,512,128]{2,1,0:T(8,128)(4,1)S(1)} %get-tuple-element.4, ...), kind=kLoop, calls=%fused_computation.177 | loop fusion | flops 19922944 | bytes 8388672 | tf_op jit(solution)/shard_map/stack | solution.py:81
  101.7 9.9 %divide_bitcast_fusion.7 = f32[1,8,512,128]{3,2,1,0:T(8,128)S(1)} fusion(f32[2,8,512,128]{3,2,1,0:T(8,128)S(1)} %copy-done.3, pred[8,512,128]{2,1,0:T(8,128)(4,1)S(1)} %get-tuple-element.6, f32[]{:T(128)} %bitcast.7, pred[8,512,128]{2,1,0:T(8,128)(4,1)S(1)} %get-tuple-element.5, f32[]{:T(128)} %bitcast.6, pred[8,512,128]{2,1,0:T(8,128)(4,1)S(1)} %get-tuple-element.4, ...), kind=kLoop, calls=%fused_computation.199 | loop fusion | flops 14155776 | bytes 6291504 | tf_op jit(solution)/shard_map/stack | solution.py:81
  127.7 11.1 %collective-permute-done.3 = f32[2,1,512,128]{3,2,1,0:T(8,128)S(1)} collective-permute-done((f32[2,1,512,128]{3,2,1,0:T(8,128)S(1)}, f32[2,1,512,128]{3,2,1,0:T(8,128)S(1)}, u32[]{:S(2)}, u32[]{:S(2)}) %collective-permute-start.3) | collective-permute-done | bytes 524320 | tf_op jit(solution)/shard_map/ppermute | solution.py:17
  138.8 13.3 %fusion.11 = f32[2,8,512,128]{3,2,1,0:T(8,128)} fusion(f32[2,8,512,128]{3,2,1,0:T(8,128)S(1)} %copy-done.3, f32[2,8,512,128]{3,2,1,0:T(8,128)} %pad_maximum_fusion.1, f32[2,1,512,128]{3,2,1,0:T(8,128)S(1)} %collective-permute-done.3, f32[1,8,512,128]{3,2,1,0:T(8,128)} %copy-done.17, f32[1,8,512,128]{3,2,1,0:T(8,128)} %copy-done.18, ...), kind=kLoop, calls=%fused_computation.74 | loop fusion | flops 14680064 | bytes 22020096 | tf_op jit(solution)/shard_map/add | solution.py:130
  152.1 15.2 %fusion.69 = f32[1,8,512,128]{3,2,1,0:T(8,128)S(1)} fusion(f32[2,8,512,128]{3,2,1,0:T(8,128)} %fusion.11, pred[8,512,128]{2,1,0:T(8,128)(4,1)S(1)} %get-tuple-element.6, f32[]{:T(128)} %bitcast.31, pred[8,512,128]{2,1,0:T(8,128)(4,1)S(1)} %get-tuple-element.5, f32[]{:T(128)} %bitcast.30, pred[8,512,128]{2,1,0:T(8,128)(4,1)S(1)} %get-tuple-element.4, ...), kind=kLoop, calls=%fused_computation.173 | loop fusion | flops 19922944 | bytes 8388672 | tf_op jit(solution)/shard_map/stack | solution.py:81
  167.3 9.9 %divide_bitcast_fusion.6 = f32[1,8,512,128]{3,2,1,0:T(8,128)S(1)} fusion(f32[2,8,512,128]{3,2,1,0:T(8,128)S(1)} %copy-done.5, pred[8,512,128]{2,1,0:T(8,128)(4,1)S(1)} %get-tuple-element.6, f32[]{:T(128)} %bitcast.7, pred[8,512,128]{2,1,0:T(8,128)(4,1)S(1)} %get-tuple-element.5, f32[]{:T(128)} %bitcast.6, pred[8,512,128]{2,1,0:T(8,128)(4,1)S(1)} %get-tuple-element.4, ...), kind=kLoop, calls=%fused_computation.197 | loop fusion | flops 14155776 | bytes 6291504 | tf_op jit(solution)/shard_map/stack | solution.py:81
  186.3 7.7 %collective-permute-done.4 = f32[2,1,512,128]{3,2,1,0:T(8,128)S(1)} collective-permute-done((f32[2,1,512,128]{3,2,1,0:T(8,128)S(1)}, f32[2,1,512,128]{3,2,1,0:T(8,128)S(1)}, u32[]{:S(2)}, u32[]{:S(2)}) %collective-permute-start.4) | collective-permute-done | bytes 524320 | tf_op jit(solution)/shard_map/ppermute | solution.py:19
  194.1 11.1 %collective-permute-done.5 = f32[2,1,512,128]{3,2,1,0:T(8,128)S(1)} collective-permute-done((f32[2,1,512,128]{3,2,1,0:T(8,128)S(1)}, f32[2,1,512,128]{3,2,1,0:T(8,128)S(1)}, u32[]{:S(2)}, u32[]{:S(2)}) %collective-permute-start.5) | collective-permute-done | bytes 524320 | tf_op jit(solution)/shard_map/ppermute | solution.py:17
  205.2 12.6 %fusion.18 = f32[2,8,512,128]{3,2,1,0:T(8,128)S(1)} fusion(f32[2,8,512,128]{3,2,1,0:T(8,128)} %fusion.11, f32[2,8,512,128]{3,2,1,0:T(8,128)} %pad_maximum_fusion.2, f32[2,1,512,128]{3,2,1,0:T(8,128)S(1)} %collective-permute-done.5, f32[1,8,512,128]{3,2,1,0:T(8,128)} %copy-done.19, f32[1,8,512,128]{3,2,1,0:T(8,128)} %copy-done.20, ...), kind=kLoop, calls=%fused_computation.81 | loop fusion | flops 14680064 | bytes 22020096 | tf_op jit(solution)/shard_map/add | solution.py:130
  217.8 13.4 %fusion.67 = f32[1,8,512,128]{3,2,1,0:T(8,128)S(1)} fusion(f32[2,8,512,128]{3,2,1,0:T(8,128)S(1)} %fusion.18, pred[8,512,128]{2,1,0:T(8,128)(4,1)S(1)} %get-tuple-element.6, f32[]{:T(128)} %bitcast.31, pred[8,512,128]{2,1,0:T(8,128)(4,1)S(1)} %get-tuple-element.5, f32[]{:T(128)} %bitcast.30, pred[8,512,128]{2,1,0:T(8,128)(4,1)S(1)} %get-tuple-element.4, ...), kind=kLoop, calls=%fused_computation.169 | loop fusion | flops 19922944 | bytes 8388672 | tf_op jit(solution)/shard_map/stack | solution.py:81
  231.2 9.9 %divide_bitcast_fusion.5 = f32[1,8,512,128]{3,2,1,0:T(8,128)S(1)} fusion(f32[2,8,512,128]{3,2,1,0:T(8,128)S(1)} %fusion.18, pred[8,512,128]{2,1,0:T(8,128)(4,1)S(1)} %get-tuple-element.6, f32[]{:T(128)} %bitcast.7, pred[8,512,128]{2,1,0:T(8,128)(4,1)S(1)} %get-tuple-element.5, f32[]{:T(128)} %bitcast.6, pred[8,512,128]{2,1,0:T(8,128)(4,1)S(1)} %get-tuple-element.4, ...), kind=kLoop, calls=%fused_computation.195 | loop fusion | flops 14155776 | bytes 6291504 | tf_op jit(solution)/shard_map/stack | solution.py:81
  250.7 7.3 %collective-permute-done.6 = f32[2,1,512,128]{3,2,1,0:T(8,128)S(1)} collective-permute-done((f32[2,1,512,128]{3,2,1,0:T(8,128)S(1)}, f32[2,1,512,128]{3,2,1,0:T(8,128)S(1)}, u32[]{:S(2)}, u32[]{:S(2)}) %collective-permute-start.6) | collective-permute-done | bytes 524320 | tf_op jit(solution)/shard_map/ppermute | solution.py:19
  257.9 11.1 %collective-permute-done.7 = f32[2,1,512,128]{3,2,1,0:T(8,128)S(1)} collective-permute-done((f32[2,1,512,128]{3,2,1,0:T(8,128)S(1)}, f32[2,1,512,128]{3,2,1,0:T(8,128)S(1)}, u32[]{:S(2)}, u32[]{:S(2)}) %collective-permute-start.7) | collective-permute-done | bytes 524320 | tf_op jit(solution)/shard_map/ppermute | solution.py:17
  269.1 12.6 %fusion.25 = f32[2,8,512,128]{3,2,1,0:T(8,128)S(1)} fusion(f32[2,8,512,128]{3,2,1,0:T(8,128)} %copy-done.4, f32[2,8,512,128]{3,2,1,0:T(8,128)} %pad_maximum_fusion.3, f32[2,1,512,128]{3,2,1,0:T(8,128)S(1)} %collective-permute-done.7, f32[1,8,512,128]{3,2,1,0:T(8,128)} %copy-done.15, f32[1,8,512,128]{3,2,1,0:T(8,128)} %copy-done.16, ...), kind=kLoop, calls=%fused_computation.88 | loop fusion | flops 14680064 | bytes 22020096 | tf_op jit(solution)/shard_map/add | solution.py:130
  283.6 47.9 %collective-permute-done.8 = f32[2,8,512,128]{3,2,1,0:T(8,128)S(1)} collective-permute-done((f32[2,8,512,128]{3,2,1,0:T(8,128)S(1)}, f32[2,8,512,128]{3,2,1,0:T(8,128)S(1)}, u32[]{:S(2)}, u32[]{:S(2)}) %collective-permute-start.8) | collective-permute-done | bytes 4194336 | tf_op jit(solution)/shard_map/ppermute | solution.py:29
  331.5 13.4 %fusion.65 = f32[1,8,512,128]{3,2,1,0:T(8,128)S(1)} fusion(f32[2,8,512,128]{3,2,1,0:T(8,128)S(1)} %collective-permute-done.8, pred[8,512,128]{2,1,0:T(8,128)(4,1)S(1)} %get-tuple-element.6, f32[]{:T(128)} %bitcast.31, pred[8,512,128]{2,1,0:T(8,128)(4,1)S(1)} %get-tuple-element.5, f32[]{:T(128)} %bitcast.30, pred[8,512,128]{2,1,0:T(8,128)(4,1)S(1)} %get-tuple-element.4, ...), kind=kLoop, calls=%fused_computation.165 | loop fusion | flops 19922944 | bytes 8388672 | tf_op jit(solution)/shard_map/stack | solution.py:81
  344.9 9.9 %divide_bitcast_fusion.2 = f32[1,8,512,128]{3,2,1,0:T(8,128)S(1)} fusion(f32[2,8,512,128]{3,2,1,0:T(8,128)S(1)} %collective-permute-done.8, pred[8,512,128]{2,1,0:T(8,128)(4,1)S(1)} %get-tuple-element.6, f32[]{:T(128)} %bitcast.7, pred[8,512,128]{2,1,0:T(8,128)(4,1)S(1)} %get-tuple-element.5, f32[]{:T(128)} %bitcast.6, ...), kind=kLoop, calls=%fused_computation.191 | loop fusion | flops 14155776 | bytes 6291504 | tf_op jit(solution)/shard_map/stack | solution.py:81
  374.4 19.9 %fusion.34 = f32[2,8,512,128]{3,2,1,0:T(8,128)} fusion(f32[2,8,512,128]{3,2,1,0:T(8,128)} %copy-done.1, f32[2,8,512,128]{3,2,1,0:T(8,128)} %copy-done.22, f32[2,8,512,128]{3,2,1,0:T(8,128)} %pad_maximum_fusion.4, f32[2,1,512,128]{3,2,1,0:T(8,128)S(1)} %collective-permute-done.10, f32[1,8,512,128]{3,2,1,0:T(8,128)} %copy-done.11, ...), kind=kLoop, calls=%fused_computation.97 | loop fusion | flops 19922944 | bytes 34603008 | tf_op jit(solution)/shard_map/jit(_where)/select_n | solution.py:139
  396.4 47.9 %collective-permute-done.11 = f32[2,8,512,128]{3,2,1,0:T(8,128)S(1)} collective-permute-done((f32[2,8,512,128]{3,2,1,0:T(8,128)}, f32[2,8,512,128]{3,2,1,0:T(8,128)S(1)}, u32[]{:S(2)}, u32[]{:S(2)}) %collective-permute-start.11) | collective-permute-done | bytes 4194336 | tf_op jit(solution)/shard_map/ppermute | solution.py:29
  444.3 13.4 %fusion.63 = f32[1,8,512,128]{3,2,1,0:T(8,128)S(1)} fusion(f32[2,8,512,128]{3,2,1,0:T(8,128)S(1)} %collective-permute-done.11, pred[8,512,128]{2,1,0:T(8,128)(4,1)S(1)} %get-tuple-element.6, f32[]{:T(128)} %bitcast.31, pred[8,512,128]{2,1,0:T(8,128)(4,1)S(1)} %get-tuple-element.5, f32[]{:T(128)} %bitcast.30, pred[8,512,128]{2,1,0:T(8,128)(4,1)S(1)} %get-tuple-element.4, ...), kind=kLoop, calls=%fused_computation.161 | loop fusion | flops 19922944 | bytes 8388672 | tf_op jit(solution)/shard_map/stack | solution.py:81
  457.8 9.9 %divide_bitcast_fusion.1 = f32[1,8,512,128]{3,2,1,0:T(8,128)S(1)} fusion(f32[2,8,512,128]{3,2,1,0:T(8,128)S(1)} %collective-permute-done.11, pred[8,512,128]{2,1,0:T(8,128)(4,1)S(1)} %get-tuple-element.6, f32[]{:T(128)} %bitcast.7, pred[8,512,128]{2,1,0:T(8,128)(4,1)S(1)} %get-tuple-element.5, f32[]{:T(128)} %bitcast.6, ...), kind=kLoop, calls=%fused_computation.189 | loop fusion | flops 14155776 | bytes 6291504 | tf_op jit(solution)/shard_map/stack | solution.py:81
  485.3 20.1 %fusion.43 = f32[2,8,512,128]{3,2,1,0:T(8,128)} fusion(f32[2,8,512,128]{3,2,1,0:T(8,128)} %fusion.34, f32[2,8,512,128]{3,2,1,0:T(8,128)} %copy-done.23, f32[2,8,512,128]{3,2,1,0:T(8,128)} %pad_maximum_fusion.5, f32[2,1,512,128]{3,2,1,0:T(8,128)S(1)} %collective-permute-done.13, f32[1,8,512,128]{3,2,1,0:T(8,128)} %copy-done.13, ...), kind=kLoop, calls=%fused_computation.106 | loop fusion | flops 19922944 | bytes 38797312 | tf_op jit(solution)/shard_map/jit(_where)/select_n | solution.py:139
  507.4 48.1 %collective-permute-done.14 = f32[2,8,512,128]{3,2,1,0:T(8,128)S(1)} collective-permute-done((f32[2,8,512,128]{3,2,1,0:T(8,128)}, f32[2,8,512,128]{3,2,1,0:T(8,128)S(1)}, u32[]{:S(2)}, u32[]{:S(2)}) %collective-permute-start.14) | collective-permute-done | bytes 4194336 | tf_op jit(solution)/shard_map/ppermute | solution.py:29
  555.5 13.4 %fusion.61 = f32[1,8,512,128]{3,2,1,0:T(8,128)S(1)} fusion(f32[2,8,512,128]{3,2,1,0:T(8,128)S(1)} %collective-permute-done.14, pred[8,512,128]{2,1,0:T(8,128)(4,1)S(1)} %get-tuple-element.6, f32[]{:T(128)} %bitcast.31, pred[8,512,128]{2,1,0:T(8,128)(4,1)S(1)} %get-tuple-element.5, f32[]{:T(128)} %bitcast.30, pred[8,512,128]{2,1,0:T(8,128)(4,1)S(1)} %get-tuple-element.4, ...), kind=kLoop, calls=%fused_computation.157 | loop fusion | flops 19922944 | bytes 8388672 | tf_op jit(solution)/shard_map/stack | solution.py:81
  568.9 9.9 %divide_bitcast_fusion = f32[1,8,512,128]{3,2,1,0:T(8,128)S(1)} fusion(f32[2,8,512,128]{3,2,1,0:T(8,128)S(1)} %collective-permute-done.14, pred[8,512,128]{2,1,0:T(8,128)(4,1)S(1)} %get-tuple-element.6, f32[]{:T(128)} %bitcast.7, pred[8,512,128]{2,1,0:T(8,128)(4,1)S(1)} %get-tuple-element.5, f32[]{:T(128)} %bitcast.6, ...), kind=kLoop, calls=%fused_computation.187 | loop fusion | flops 14155776 | bytes 6291504 | tf_op jit(solution)/shard_map/stack | solution.py:81
  596.5 19.5 %fusion.52 = f32[2,8,512,128]{3,2,1,0:T(8,128)} fusion(f32[2,8,512,128]{3,2,1,0:T(8,128)} %fusion.43, f32[2,8,512,128]{3,2,1,0:T(8,128)} %copy-done.21, f32[2,8,512,128]{3,2,1,0:T(8,128)} %pad_maximum_fusion.6, f32[2,1,512,128]{3,2,1,0:T(8,128)S(1)} %collective-permute-done.16, f32[1,8,512,128]{3,2,1,0:T(8,128)} %copy-done.7, ...), kind=kLoop, calls=%fused_computation.115 | loop fusion | flops 19922944 | bytes 38797312 | tf_op jit(solution)/shard_map/jit(_where)/select_n | solution.py:139
  (106 shorter events, 121.5 us)
Async XLA Ops:
  29.3 20.7 %copy-start.9 = (f32[1,8,512,128]{3,2,1,0:T(8,128)}, f32[1,8,512,128]{3,2,1,0:T(8,128)S(1)}, u32[]{:S(2)}) copy-start(f32[1,8,512,128]{3,2,1,0:T(8,128)S(1)} %fusion.76) | copy-start | bytes 6291460
  42.8 28.6 %collective-permute-start = (f32[2,1,512,128]{3,2,1,0:T(8,128)S(1)}, f32[2,1,512,128]{3,2,1,0:T(8,128)S(1)}, u32[]{:S(2)}, u32[]{:S(2)}) collective-permute-start(f32[2,1,512,128]{3,2,1,0:T(8,128)S(1)} %get-tuple-element.23), channel_id=1, source_target_pairs={{1,0},{2,1},{3,2},{4,3},{5,4},{6,5},{7,6},{9,8},{10,9},{11,10},{12... | collective-permute-start | bytes 1572872 | tf_op jit(solution)/shard_map/ppermute | solution.py:19
  45.3 26.2 %collective-permute-start.1 = (f32[2,1,512,128]{3,2,1,0:T(8,128)S(1)}, f32[2,1,512,128]{3,2,1,0:T(8,128)S(1)}, u32[]{:S(2)}, u32[]{:S(2)}) collective-permute-start(f32[2,1,512,128]{3,2,1,0:T(8,128)S(1)} %get-tuple-element.24), channel_id=1, source_target_pairs={{0,1},{1,2},{2,3},{3,4},{4,5},{5,6},{6,7},{8,9},{9,10},{10,11},{11... | collective-permute-start | bytes 1572872 | tf_op jit(solution)/shard_map/ppermute | solution.py:17
  53.1 18.3 %copy-start = (f32[2,8,512,128]{3,2,1,0:T(8,128)}, f32[2,8,512,128]{3,2,1,0:T(8,128)S(1)}, u32[]{:S(2)}) copy-start(f32[2,8,512,128]{3,2,1,0:T(8,128)S(1)} %constant_dynamic-update-slice_fusion) | copy-start | bytes 12582916
  86.4 15.3 %copy-start.3 = (f32[2,8,512,128]{3,2,1,0:T(8,128)S(1)}, f32[2,8,512,128]{3,2,1,0:T(8,128)}, u32[]{:S(2)}) copy-start(f32[2,8,512,128]{3,2,1,0:T(8,128)} %get-tuple-element.7) | copy-start | bytes 12582916
  101.7 17.1 %copy-start.17 = (f32[1,8,512,128]{3,2,1,0:T(8,128)}, f32[1,8,512,128]{3,2,1,0:T(8,128)S(1)}, u32[]{:S(2)}) copy-start(f32[1,8,512,128]{3,2,1,0:T(8,128)S(1)} %fusion.71) | copy-start | bytes 6291460
  111.7 16.0 %collective-permute-start.2 = (f32[2,1,512,128]{3,2,1,0:T(8,128)S(1)}, f32[2,1,512,128]{3,2,1,0:T(8,128)S(1)}, u32[]{:S(2)}, u32[]{:S(2)}) collective-permute-start(f32[2,1,512,128]{3,2,1,0:T(8,128)S(1)} %get-tuple-element.21), channel_id=1, source_target_pairs={{1,0},{2,1},{3,2},{4,3},{5,4},{6,5},{7,6},{9,8},{10,9},{11,10},{12... | collective-permute-start | bytes 1572872 | tf_op jit(solution)/shard_map/ppermute | solution.py:19
  113.6 25.2 %copy-start.2 = (f32[1,8,512,128]{3,2,1,0:T(8,128)S(1)}, f32[1,8,512,128]{3,2,1,0:T(8,128)}, u32[]{:S(2)}) copy-start(f32[1,8,512,128]{3,2,1,0:T(8,128)} %fusion.78) | copy-start | bytes 6291460
  113.6 25.2 %collective-permute-start.3 = (f32[2,1,512,128]{3,2,1,0:T(8,128)S(1)}, f32[2,1,512,128]{3,2,1,0:T(8,128)S(1)}, u32[]{:S(2)}, u32[]{:S(2)}) collective-permute-start(f32[2,1,512,128]{3,2,1,0:T(8,128)S(1)} %get-tuple-element.22), channel_id=1, source_target_pairs={{0,1},{1,2},{2,3},{3,4},{4,5},{5,6},{6,7},{8,9},{9,10},{10,11},{11... | collective-permute-start | bytes 1572872 | tf_op jit(solution)/shard_map/ppermute | solution.py:17
  152.1 15.2 %copy-start.5 = (f32[2,8,512,128]{3,2,1,0:T(8,128)S(1)}, f32[2,8,512,128]{3,2,1,0:T(8,128)}, u32[]{:S(2)}) copy-start(f32[2,8,512,128]{3,2,1,0:T(8,128)} %fusion.11) | copy-start | bytes 12582916
  167.3 16.7 %copy-start.19 = (f32[1,8,512,128]{3,2,1,0:T(8,128)}, f32[1,8,512,128]{3,2,1,0:T(8,128)S(1)}, u32[]{:S(2)}) copy-start(f32[1,8,512,128]{3,2,1,0:T(8,128)S(1)} %fusion.69) | copy-start | bytes 6291460
  177.3 16.7 %collective-permute-start.4 = (f32[2,1,512,128]{3,2,1,0:T(8,128)S(1)}, f32[2,1,512,128]{3,2,1,0:T(8,128)S(1)}, u32[]{:S(2)}, u32[]{:S(2)}) collective-permute-start(f32[2,1,512,128]{3,2,1,0:T(8,128)S(1)} %get-tuple-element.19), channel_id=1, source_target_pairs={{1,0},{2,1},{3,2},{4,3},{5,4},{6,5},{7,6},{9,8},{10,9},{11,10},{12... | collective-permute-start | bytes 1572872 | tf_op jit(solution)/shard_map/ppermute | solution.py:19
  179.3 25.9 %collective-permute-start.5 = (f32[2,1,512,128]{3,2,1,0:T(8,128)S(1)}, f32[2,1,512,128]{3,2,1,0:T(8,128)S(1)}, u32[]{:S(2)}, u32[]{:S(2)}) collective-permute-start(f32[2,1,512,128]{3,2,1,0:T(8,128)S(1)} %get-tuple-element.20), channel_id=1, source_target_pairs={{0,1},{1,2},{2,3},{3,4},{4,5},{5,6},{6,7},{8,9},{9,10},{10,11},{11... | collective-permute-start | bytes 1572872 | tf_op jit(solution)/shard_map/ppermute | solution.py:17
  217.8 13.4 %copy-start.4 = (f32[2,8,512,128]{3,2,1,0:T(8,128)}, f32[2,8,512,128]{3,2,1,0:T(8,128)S(1)}, u32[]{:S(2)}) copy-start(f32[2,8,512,128]{3,2,1,0:T(8,128)S(1)} %fusion.18) | copy-start | bytes 12582916
  231.2 17.2 %copy-start.15 = (f32[1,8,512,128]{3,2,1,0:T(8,128)}, f32[1,8,512,128]{3,2,1,0:T(8,128)S(1)}, u32[]{:S(2)}) copy-start(f32[1,8,512,128]{3,2,1,0:T(8,128)S(1)} %fusion.67) | copy-start | bytes 6291460
  241.2 16.7 %collective-permute-start.6 = (f32[2,1,512,128]{3,2,1,0:T(8,128)S(1)}, f32[2,1,512,128]{3,2,1,0:T(8,128)S(1)}, u32[]{:S(2)}, u32[]{:S(2)}) collective-permute-start(f32[2,1,512,128]{3,2,1,0:T(8,128)S(1)} %get-tuple-element.17), channel_id=1, source_target_pairs={{1,0},{2,1},{3,2},{4,3},{5,4},{6,5},{7,6},{9,8},{10,9},{11,10},{12... | collective-permute-start | bytes 1572872 | tf_op jit(solution)/shard_map/ppermute | solution.py:19
  243.1 25.9 %collective-permute-start.7 = (f32[2,1,512,128]{3,2,1,0:T(8,128)S(1)}, f32[2,1,512,128]{3,2,1,0:T(8,128)S(1)}, u32[]{:S(2)}, u32[]{:S(2)}) collective-permute-start(f32[2,1,512,128]{3,2,1,0:T(8,128)S(1)} %get-tuple-element.18), channel_id=1, source_target_pairs={{0,1},{1,2},{2,3},{3,4},{4,5},{5,6},{6,7},{8,9},{9,10},{10,11},{11... | collective-permute-start | bytes 1572872 | tf_op jit(solution)/shard_map/ppermute | solution.py:17
  281.6 63.3 %copy-start.1 = (f32[2,8,512,128]{3,2,1,0:T(8,128)}, f32[2,8,512,128]{3,2,1,0:T(8,128)S(1)}, u32[]{:S(2)}) copy-start(f32[2,8,512,128]{3,2,1,0:T(8,128)S(1)} %fusion.25) | copy-start | bytes 12582916
  281.7 49.8 %collective-permute-start.8 = (f32[2,8,512,128]{3,2,1,0:T(8,128)S(1)}, f32[2,8,512,128]{3,2,1,0:T(8,128)S(1)}, u32[]{:S(2)}, u32[]{:S(2)}) collective-permute-start(f32[2,8,512,128]{3,2,1,0:T(8,128)S(1)} %fusion.25), channel_id=1, source_target_pairs={{0,8},{8,16},{16,24},{1,9},{9,17},{17,25},{2,10},{10,18},{18,26},{... | collective-permute-start | bytes 12582920 | tf_op jit(solution)/shard_map/ppermute | solution.py:29
  331.5 13.4 %copy-start.22 = (f32[2,8,512,128]{3,2,1,0:T(8,128)}, f32[2,8,512,128]{3,2,1,0:T(8,128)S(1)}, u32[]{:S(2)}) copy-start(f32[2,8,512,128]{3,2,1,0:T(8,128)S(1)} %collective-permute-done.8) | copy-start | bytes 12582916
  356.6 12.3 %collective-permute-start.9 = (f32[2,1,512,128]{3,2,1,0:T(8,128)}, f32[2,1,512,128]{3,2,1,0:T(8,128)S(1)}, u32[]{:S(2)}, u32[]{:S(2)}) collective-permute-start(f32[2,1,512,128]{3,2,1,0:T(8,128)} %get-tuple-element.15), channel_id=1, source_target_pairs={{1,0},{2,1},{3,2},{4,3},{5,4},{6,5},{7,6},{9,8},{10,9},{11,10},{12... | collective-permute-start | bytes 1572872 | tf_op jit(solution)/shard_map/ppermute | solution.py:19
  358.5 15.9 %collective-permute-start.10 = (f32[2,1,512,128]{3,2,1,0:T(8,128)}, f32[2,1,512,128]{3,2,1,0:T(8,128)S(1)}, u32[]{:S(2)}, u32[]{:S(2)}) collective-permute-start(f32[2,1,512,128]{3,2,1,0:T(8,128)} %get-tuple-element.16), channel_id=1, source_target_pairs={{0,1},{1,2},{2,3},{3,4},{4,5},{5,6},{6,7},{8,9},{9,10},{10,11},{11... | collective-permute-start | bytes 1572872 | tf_op jit(solution)/shard_map/ppermute | solution.py:17
  394.3 50.0 %collective-permute-start.11 = (f32[2,8,512,128]{3,2,1,0:T(8,128)}, f32[2,8,512,128]{3,2,1,0:T(8,128)S(1)}, u32[]{:S(2)}, u32[]{:S(2)}) collective-permute-start(f32[2,8,512,128]{3,2,1,0:T(8,128)} %fusion.34), channel_id=1, source_target_pairs={{0,8},{8,16},{16,24},{1,9},{9,17},{17,25},{2,10},{10,18},{18,26},{... | collective-permute-start | bytes 12582920 | tf_op jit(solution)/shard_map/ppermute | solution.py:29
  444.3 13.4 %copy-start.23 = (f32[2,8,512,128]{3,2,1,0:T(8,128)}, f32[2,8,512,128]{3,2,1,0:T(8,128)S(1)}, u32[]{:S(2)}) copy-start(f32[2,8,512,128]{3,2,1,0:T(8,128)S(1)} %collective-permute-done.11) | copy-start | bytes 12582916
  457.7 16.7 %copy-start.13 = (f32[1,8,512,128]{3,2,1,0:T(8,128)}, f32[1,8,512,128]{3,2,1,0:T(8,128)S(1)}, u32[]{:S(2)}) copy-start(f32[1,8,512,128]{3,2,1,0:T(8,128)S(1)} %fusion.63) | copy-start | bytes 6291460
  467.7 12.1 %collective-permute-start.12 = (f32[2,1,512,128]{3,2,1,0:T(8,128)S(1)}, f32[2,1,512,128]{3,2,1,0:T(8,128)S(1)}, u32[]{:S(2)}, u32[]{:S(2)}) collective-permute-start(f32[2,1,512,128]{3,2,1,0:T(8,128)S(1)} %get-tuple-element.13), channel_id=1, source_target_pairs={{1,0},{2,1},{3,2},{4,3},{5,4},{6,5},{7,6},{9,8},{10,9},{11,10},{12... | collective-permute-start | bytes 1572872 | tf_op jit(solution)/shard_map/ppermute | solution.py:19
  469.7 15.7 %collective-permute-start.13 = (f32[2,1,512,128]{3,2,1,0:T(8,128)S(1)}, f32[2,1,512,128]{3,2,1,0:T(8,128)S(1)}, u32[]{:S(2)}, u32[]{:S(2)}) collective-permute-start(f32[2,1,512,128]{3,2,1,0:T(8,128)S(1)} %get-tuple-element.14), channel_id=1, source_target_pairs={{0,1},{1,2},{2,3},{3,4},{4,5},{5,6},{6,7},{8,9},{9,10},{10,11},{11... | collective-permute-start | bytes 1572872 | tf_op jit(solution)/shard_map/ppermute | solution.py:17
  505.5 50.0 %collective-permute-start.14 = (f32[2,8,512,128]{3,2,1,0:T(8,128)}, f32[2,8,512,128]{3,2,1,0:T(8,128)S(1)}, u32[]{:S(2)}, u32[]{:S(2)}) collective-permute-start(f32[2,8,512,128]{3,2,1,0:T(8,128)} %fusion.43), channel_id=1, source_target_pairs={{0,8},{8,16},{16,24},{1,9},{9,17},{17,25},{2,10},{10,18},{18,26},{... | collective-permute-start | bytes 12582920 | tf_op jit(solution)/shard_map/ppermute | solution.py:29
  568.9 17.1 %copy-start.7 = (f32[1,8,512,128]{3,2,1,0:T(8,128)}, f32[1,8,512,128]{3,2,1,0:T(8,128)S(1)}, u32[]{:S(2)}) copy-start(f32[1,8,512,128]{3,2,1,0:T(8,128)S(1)} %fusion.61) | copy-start | bytes 6291460
  578.9 12.1 %collective-permute-start.15 = (f32[2,1,512,128]{3,2,1,0:T(8,128)S(1)}, f32[2,1,512,128]{3,2,1,0:T(8,128)S(1)}, u32[]{:S(2)}, u32[]{:S(2)}) collective-permute-start(f32[2,1,512,128]{3,2,1,0:T(8,128)S(1)} %get-tuple-element.11), channel_id=1, source_target_pairs={{1,0},{2,1},{3,2},{4,3},{5,4},{6,5},{7,6},{9,8},{10,9},{11,10},{12... | collective-permute-start | bytes 1572872 | tf_op jit(solution)/shard_map/ppermute | solution.py:19
  580.9 15.7 %copy-start.6 = (f32[1,8,512,128]{3,2,1,0:T(8,128)S(1)}, f32[1,8,512,128]{3,2,1,0:T(8,128)}, u32[]{:S(2)}) copy-start(f32[1,8,512,128]{3,2,1,0:T(8,128)} %get-tuple-element.25) | copy-start | bytes 6291460
  580.9 15.7 %collective-permute-start.16 = (f32[2,1,512,128]{3,2,1,0:T(8,128)S(1)}, f32[2,1,512,128]{3,2,1,0:T(8,128)S(1)}, u32[]{:S(2)}, u32[]{:S(2)}) collective-permute-start(f32[2,1,512,128]{3,2,1,0:T(8,128)S(1)} %get-tuple-element.12), channel_id=1, source_target_pairs={{0,1},{1,2},{2,3},{3,4},{4,5},{5,6},{6,7},{8,9},{9,10},{10,11},{11... | collective-permute-start | bytes 1572872 | tf_op jit(solution)/shard_map/ppermute | solution.py:17
  (13 other events, 92.9 us)
where the time goes:
time: 628 us; the launch traced here: 621 us
  other arithmetic  325 us (52%)
  waiting for transfers between devices  222 us (35%)
  starting transfers between devices  54.5 us (9%)
  local copies, waits for them, and re-layouts  17.4 us (3%)
    another operation x28, other arithmetic, fractions(): jnp.stack([local_warmth_value, gridded_quantities[1] / denominator_quanti...  187 us
    ppermute x3, waiting for transfers between devices, shifted(): return lax.ppermute(x, axis, pairs)  144 us
    select_n x3, other arithmetic, per_device(): result = jnp.where(position == 0, result, predicted + correction)  59.5 us
    add x4, other arithmetic, per_device(): gridded_quantities = gridded_quantities + rate_pair * laplacian  53.4 us
    ppermute x7, waiting for transfers between devices, with_halo(): lax.ppermute(tail, axis, [(i, (i + 1) % count) for i in range(ends)])  49.9 us
    ppermute x7, starting transfers between devices, with_halo(): lax.ppermute(tail, axis, [(i, (i + 1) % count) for i in range(ends)])  34.7 us
    ppermute x7, waiting for transfers between devices, with_halo(): lax.ppermute(head, axis, [((i + 1) % count, i) for i in range(ends)])  28.1 us
    another operation x2, other arithmetic, coefficients(): jnp.stack([4.0 * heat_gain / (1.0 + 18.0 * thermal_ratio), 4.0 * solute_g...  17.7 us
  transfers between devices with their start and end apart: 17, of which 15 were waited for; matrix products, arithmetic and copies ran while one was open for 6% of the time, Pallas kernels for 0%

commit v1 on v0

v1 whole, which is shorter than its diff:
```python
import functools

import jax
import jax.numpy as jnp
from jax import lax
from jax.experimental import pallas as pl
from jax.experimental.pallas import tpu as pltpu
from jax.sharding import PartitionSpec as P

STEPS = 4
CHUNK = 64
MIB = 1024 * 1024
SMEM = pl.BlockSpec(memory_space=pltpu.SMEM)
VMEM = pl.BlockSpec(memory_space=pltpu.VMEM)


class Tables:
    def __init__(self, prm):
        def raw(first, count):
            return [jnp.full((8, 128), prm[first + m], jnp.float32) for m in range(count)]

        cap, self.lat, self.hs = raw(0, 4), raw(4, 4), raw(8, 4)
        kp, bd, xr = raw(12, 4), raw(16, 4), raw(20, 4)
        self.sg = raw(24, 3)
        q = [(1.0 - k) / (1.0 + b) for k, b in zip(kp, bd)]
        self.icap = [1.0 / c for c in cap]
        self.den0 = [1.0 - v for v in q]
        self.den1 = [v / t for v, t in zip(q, self.lat)]
        self.hg = [x * c for x, c in zip(xr, cap)]
        self.gh = [4.0 / (1.0 + 18.0 * x) for x in xr]
        self.crh = [h * g for h, g in zip(self.hg, self.gh)]
        self.kp18 = [18.0 / k for k in kp]


class Cells:
    def __init__(self, tab, ids):
        self.tab, self.shape = tab, ids.shape
        self.b0 = (ids & 1) != 0
        self.b1 = (ids & 2) != 0
        self.p1 = (ids & 4) != 0
        self.p2 = (ids & 8) != 0

    def wide(self, tile):
        reps = self.shape[0] // 8
        return jnp.broadcast_to(tile[None], (reps, 8, 128)).reshape(self.shape)

    def alloy(self, name):
        t = [self.wide(v) for v in getattr(self.tab, name)]
        return jnp.where(self.b1, jnp.where(self.b0, t[3], t[2]), jnp.where(self.b0, t[1], t[0]))

    def solute_gain(self):
        t = [self.wide(v) for v in self.tab.sg]
        return jnp.where(self.p2, t[2], jnp.where(self.p1, t[1], t[0]))

    def fine(self):
        return self.alloy("hg"), self.solute_gain()

    def ratio(self):
        sg = self.solute_gain()
        return self.alloy("gh"), 4.0 / (1.0 + sg * self.alloy("kp18"))

    def coarse(self):
        sg = self.solute_gain()
        return self.alloy("crh"), 4.0 * sg / (1.0 + sg * self.alloy("kp18"))

    def melt(self, h, c):
        sensible = h - self.alloy("hs")
        held = jnp.minimum(jnp.maximum(sensible, 0.0), self.alloy("lat"))
        t = (h - held) * self.alloy("icap")
        return t, c / (self.alloy("den0") + self.alloy("den1") * held)


def chunks(ny, body):
    step = min(CHUNK, ny)

    def run(i, carry):
        body(pl.multiple_of(i * step, step), step)
        return carry

    lax.fori_loop(0, ny // step, run, 0)


def clear_rims(pad, ny):
    rows = pad.shape[1]
    for f in range(2):
        for r in range(rows):
            pad[f, r, 0:8, :] = jnp.zeros((8, 128), jnp.float32)
            pad[f, r, 8 + ny : 16 + ny, :] = jnp.zeros((8, 128), jnp.float32)


def put_melt(pad, r, y, n, cells, h, c):
    t, l = cells.melt(h, c)
    pad[0, r, pl.ds(y + 8, n), :] = t
    pad[1, r, pl.ds(y + 8, n), :] = l


def lap(pad, f, r, y, n, below, above):
    ext = pad[f, r, pl.ds(y, n + 16), :]
    mid = ext[8 : 8 + n]
    lane = lax.broadcasted_iota(jnp.int32, (n, 128), 1)
    total = pltpu.roll(ext, 1, 0)[8 : 8 + n] + pltpu.roll(ext, n + 15, 0)[8 : 8 + n]
    total = total + jnp.where(lane == 0, 0.0, pltpu.roll(mid, 1, 1))
    total = total + jnp.where(lane == 127, 0.0, pltpu.roll(mid, 127, 1))
    total = total - 6.0 * mid
    if below:
        total = total + pad[f, r - 1, pl.ds(y + 8, n), :]
    if above:
        total = total + pad[f, r + 1, pl.ds(y + 8, n), :]
    return total


def first_edges_kernel(prm, h, c, mat, ph, tl0, tl7):
    tab = Tables(prm)
    ny = h.shape[1]
    side = pl.program_id(0)

    def body(y, n):
        s = pl.ds(y, n)
        cells = Cells(tab, mat[0, s, :])
        t, l = cells.melt(h[0, s, :], c[0, s, :])

        @pl.when(side == 0)
        def _():
            tl0[0, s, :] = t
            tl0[1, s, :] = l

        @pl.when(side == 1)
        def _():
            tl7[0, s, :] = t
            tl7[1, s, :] = l

    chunks(ny, body)


def first_step_kernel(prm, h, c, mat, ph, hm, cm, part, idm, ide, pad):
    tab = Tables(prm)
    rows, ny = h.shape[0], h.shape[1]
    clear_rims(pad, ny)

    def melt_row(r):
        def body(y, n):
            s = pl.ds(y, n)
            ids = mat[r, s, :] + 4 * ph[r, s, :]
            put_melt(pad, r, y, n, Cells(tab, ids), h[r, s, :], c[r, s, :])
            if r == 0:
                ide[0, s, :] = ids
            elif r == rows - 1:
                ide[1, s, :] = ids
            else:
                idm[r - 1, s, :] = ids

        chunks(ny, body)

    def step_row(r):
        def body(y, n):
            s = pl.ds(y, n)
            ids = mat[r, s, :] + 4 * ph[r, s, :]
            rh, rc = Cells(tab, ids).fine()
            nh = h[r, s, :] + rh * lap(pad, 0, r, y, n, r > 0, r < rows - 1)
            nc = c[r, s, :] + rc * lap(pad, 1, r, y, n, r > 0, r < rows - 1)
            if 0 < r < rows - 1:
                hm[r - 1, s, :] = nh
                cm[r - 1, s, :] = nc
            else:
                part[min(r, 1), 0, s, :] = nh
                part[min(r, 1), 1, s, :] = nc

        chunks(ny, body)

    for r in range(rows):
        melt_row(r)
    for r in range(rows):
        step_row(r)


def step_kernel(prm, hm, cm, edge, idm, ide, nhm, ncm, part, pad):
    tab = Tables(prm)
    rows, ny = hm.shape[0] + 2, hm.shape[1]
    clear_rims(pad, ny)

    def load(r, s):
        if 0 < r < rows - 1:
            return hm[r - 1, s, :], cm[r - 1, s, :], idm[r - 1, s, :]
        e = min(r, 1)
        return edge[e, 0, s, :], edge[e, 1, s, :], ide[e, s, :]

    def melt_row(r):
        def body(y, n):
            h, c, ids = load(r, pl.ds(y, n))
            put_melt(pad, r, y, n, Cells(tab, ids), h, c)

        chunks(ny, body)

    def step_row(r):
        def body(y, n):
            s = pl.ds(y, n)
            h, c, ids = load(r, s)
            rh, rc = Cells(tab, ids).fine()
            nh = h + rh * lap(pad, 0, r, y, n, r > 0, r < rows - 1)
            nc = c + rc * lap(pad, 1, r, y, n, r > 0, r < rows - 1)
            if 0 < r < rows - 1:
                nhm[r - 1, s, :] = nh
                ncm[r - 1, s, :] = nc
            else:
                part[min(r, 1), 0, s, :] = nh
                part[min(r, 1), 1, s, :] = nc

        chunks(ny, body)

    for r in range(rows):
        melt_row(r)
    for r in range(rows):
        step_row(r)


def edges_kernel(prm, part, low, high, ide, edge, tl0, tl7):
    tab = Tables(prm)
    for e, (halo, tl) in enumerate(((low, tl0), (high, tl7))):

        def body(y, n):
            s = pl.ds(y, n)
            cells = Cells(tab, ide[e, s, :])
            rh, rc = cells.fine()
            h = part[e, 0, s, :] + rh * halo[0, s, :]
            c = part[e, 1, s, :] + rc * halo[1, s, :]
            edge[e, 0, s, :] = h
            edge[e, 1, s, :] = c
            t, l = cells.melt(h, c)
            tl[0, s, :] = t
            tl[1, s, :] = l

        chunks(part.shape[2], body)


def coarse_edges_kernel(own, prm, part, low, high, ide, old, edge, tl0, tl7):
    tab = Tables(prm)
    mine = own[0] != 0

    @pl.when(mine)
    def _():
        for e, (halo, tl) in enumerate(((low, tl0), (high, tl7))):

            def body(y, n):
                s = pl.ds(y, n)
                cells = Cells(tab, ide[e, s, :])
                rh, rc = cells.coarse()
                h = part[e, 0, s, :] + rh * halo[0, s, :]
                c = part[e, 1, s, :] + rc * halo[1, s, :]
                edge[e, 0, s, :] = h
                edge[e, 1, s, :] = c
                t, l = cells.melt(h, c)
                tl[0, s, :] = t
                tl[1, s, :] = l

            chunks(part.shape[2], body)

    @pl.when(jnp.logical_not(mine))
    def _():
        edge[...] = old[...]


def last_edges_kernel(own, prm, part, low, high, ide, old, oh, oc, nh, nc):
    tab = Tables(prm)
    mine = own[0] != 0
    side = pl.program_id(0)

    @pl.when(mine)
    def _():
        def body(y, n):
            s = pl.ds(y, n)
            cells = Cells(tab, ide[0, s, :])
            rh, rc = cells.coarse()
            ht = jnp.where(side == 0, low[0, s, :], high[0, s, :])
            hl = jnp.where(side == 0, low[1, s, :], high[1, s, :])
            nh[0, 0, s, :] = part[0, 0, s, :] + rh * ht
            nc[0, 0, s, :] = part[0, 1, s, :] + rc * hl

        chunks(part.shape[2], body)

    @pl.when(jnp.logical_not(mine))
    def _():
        nh[0, 0] = old[0, 0]
        nc[0, 0] = old[0, 1]


def drift_kernel(prm, h4, c4, h0, c0, h1, c1, ids, dh, dc):
    tab = Tables(prm)

    def body(y, n):
        s = pl.ds(y, n)
        gh, gc = Cells(tab, ids[0, s, :]).ratio()
        u, v = h0[0, s, :], c0[0, s, :]
        dh[0, s, :] = h4[0, s, :] - u - gh * (h1[0, s, :] - u)
        dc[0, s, :] = c4[0, s, :] - v - gc * (c1[0, s, :] - v)

    chunks(h4.shape[1], body)


def drift_edges_kernel(prm, e4, h0, c0, e1, ids, de):
    tab = Tables(prm)

    def body(y, n):
        s = pl.ds(y, n)
        gh, gc = Cells(tab, ids[0, s, :]).ratio()
        u, v = h0[0, s, :], c0[0, s, :]
        de[0, 0, s, :] = e4[0, 0, s, :] - u - gh * (e1[0, 0, s, :] - u)
        de[0, 1, s, :] = e4[0, 1, s, :] - v - gc * (e1[0, 1, s, :] - v)

    chunks(e4.shape[2], body)


def coarse_mid_kernel(own, prm, vm, vn, dhm, dcm, idm, old, new, pad):
    tab = Tables(prm)
    mine = own[0] != 0
    mid, ny = vm.shape[1], vm.shape[2]

    @pl.when(mine)
    def _():
        clear_rims(pad, ny)

        def load(r, s):
            if 0 < r < mid + 1:
                return vm[0, r - 1, s, :], vm[1, r - 1, s, :]
            return vn[0, min(r, 1), s, :], vn[1, min(r, 1), s, :]

        for r in range(mid + 2):

            def body(y, n):
                s = pl.ds(y, n)
                h, c = load(r, s)
                put_melt(pad, r, y, n, Cells(tab, idm[r, s, :]), h, c)

            chunks(ny, body)
        for r in range(1, mid + 1):

            def body2(y, n):
                s = pl.ds(y, n)
                h, c = load(r, s)
                rh, rc = Cells(tab, idm[r, s, :]).coarse()
                new[0, r - 1, s, :] = h + dhm[r, s, :] + rh * lap(pad, 0, r, y, n, True, True)
                new[1, r - 1, s, :] = c + dcm[r, s, :] + rc * lap(pad, 1, r, y, n, True, True)

            chunks(ny, body2)

    @pl.when(jnp.logical_not(mine))
    def _():
        new[...] = old[...]


def coarse_rim_kernel(own, prm, vo, vn, vm, dhm, dcm, de, idm, ide, old, new, part, pad):
    tab = Tables(prm)
    mine = own[0] != 0
    mid, ny = vm.shape[1], vm.shape[2]

    @pl.when(mine)
    def _():
        clear_rims(pad, ny)
        for e in range(2):
            near, far = (0, mid - 1)[e], (1, mid)[e]

            def load(k, s):
                if k == 0:
                    return vo[e, 0, s, :], vo[e, 1, s, :], ide[e, s, :]
                if k == 1:
                    return vn[0, e, s, :], vn[1, e, s, :], idm[e * (mid + 1), s, :]
                row = e * (mid - 1)
                return vm[0, row, s, :], vm[1, row, s, :], idm[row + 1, s, :]

            for k in range(3):

                def body(y, n):
                    h, c, ids = load(k, pl.ds(y, n))
                    put_melt(pad, 3 * e + k, y, n, Cells(tab, ids), h, c)

                chunks(ny, body)
            for k in range(2):

                def body2(y, n):
                    s = pl.ds(y, n)
                    h, c, ids = load(k, s)
                    rh, rc = Cells(tab, ids).coarse()
                    h = h + rh * lap(pad, 0, 3 * e + k, y, n, k > 0, True)
                    c = c + rc * lap(pad, 1, 3 * e + k, y, n, k > 0, True)
                    if k == 0:
                        part[e, 0, s, :] = h + de[e, 0, s, :]
                        part[e, 1, s, :] = c + de[e, 1, s, :]
                    else:
                        new[0, e, s, :] = h + dhm[e * (mid + 1), s, :]
                        new[1, e, s, :] = c + dcm[e * (mid + 1), s, :]

                chunks(ny, body2)

    @pl.when(jnp.logical_not(mine))
    def _():
        new[...] = old[...]


def spread_kernel(vm, vn, oh, oc):
    mid = vm.shape[1]
    for f, out in enumerate((oh, oc)):
        out[0, 1] = vn[f, 0]
        out[0, mid + 2] = vn[f, 1]
        for r in range(mid):
            out[0, 2 + r] = vm[f, r]


def f32(*shape):
    return jax.ShapeDtypeStruct(shape, jnp.float32)


def i32(*shape):
    return jax.ShapeDtypeStruct(shape, jnp.int32)


def call(kernel, outs, args, smem, cells, scratch=(), limit=32, name=None):
    nbytes = 4 * sum(a.size for a in args) + 4 * sum(o.size for o in outs)
    return pl.pallas_call(
        kernel,
        out_shape=outs,
        in_specs=[SMEM] * smem + [VMEM] * (len(args) - smem),
        out_specs=[VMEM] * len(outs),
        scratch_shapes=scratch,
        compiler_params=pltpu.CompilerParams(vmem_limit_bytes=limit * MIB),
        cost_estimate=pl.CostEstimate(flops=100 * cells, bytes_accessed=nbytes, transcendentals=0),
        name=name,
    )(*args)


def per_device(slices, parts, enthalpy, solute, material, phase_flag, *params):
    rows, ny, nz = material.shape
    mid = rows - 4
    row = ny * nz
    h0 = enthalpy.reshape(rows, ny, nz)
    c0 = solute.reshape(rows, ny, nz)
    prm = jnp.concatenate(params)
    slot = lax.axis_index("tm")

    def pad(n):
        return [pltpu.VMEM((2, n, ny + 16, nz), jnp.float32)]

    def move(x, tms, up, by):
        pairs = [
            (t * parts + s, (t + up) * parts + s + by)
            for t in tms
            for s in range(parts)
            if 0 <= s + by < parts
        ]
        return lax.ppermute(x, ("tm", "space"), pairs)

    def halos(tl0, tl7, tms, up):
        return move(tl7, tms, up, 1), move(tl0, tms, up, -1)

    edge_rows = pl.BlockSpec((1, ny, nz), lambda i: ((rows - 1) * i, 0, 0))
    whole = pl.BlockSpec((2, ny, nz), lambda i: (0, 0, 0))
    tl0, tl7 = pl.pallas_call(
        first_edges_kernel,
        grid=(2,),
        out_shape=[f32(2, ny, nz)] * 2,
        in_specs=[SMEM] + [edge_rows] * 4,
        out_specs=[whole] * 2,
        compiler_params=pltpu.CompilerParams(vmem_limit_bytes=16 * MIB),
        name="first_edges",
    )(prm, h0, c0, material, phase_flag)

    every = range(slices)
    low, high = halos(tl0, tl7, every, 0)
    hm, cm, part, idm, ide = call(
        first_step_kernel,
        [f32(rows - 2, ny, nz)] * 2 + [f32(2, 2, ny, nz), i32(rows - 2, ny, nz), i32(2, ny, nz)],
        (prm, h0, c0, material, phase_flag),
        1,
        rows * row,
        pad(rows),
        40,
        "first_step",
    )
    h1, c1 = hm, cm
    e1 = None
    for k in range(STEPS):
        edge, tl0, tl7 = call(
            edges_kernel,
            [f32(2, 2, ny, nz)] + [f32(2, ny, nz)] * 2,
            (prm, part, low, high, ide),
            1,
            2 * row,
            limit=16,
            name="edges",
        )
        if k == 0:
            e1 = edge
        if k < STEPS - 1:
            low, high = halos(tl0, tl7, every, 0)
            hm, cm, part = call(
                step_kernel,
                [f32(rows - 2, ny, nz)] * 2 + [f32(2, 2, ny, nz)],
                (prm, hm, cm, edge, idm, ide),
                1,
                rows * row,
                pad(rows),
                40,
                "step",
            )

    one = pl.BlockSpec((1, ny, nz), lambda i: (i, 0, 0))
    inner = pl.BlockSpec((1, ny, nz), lambda i: (i + 1, 0, 0))
    dhm, dcm = pl.pallas_call(
        drift_kernel,
        grid=(rows - 2,),
        out_shape=[f32(rows - 2, ny, nz)] * 2,
        in_specs=[SMEM, one, one, inner, inner, one, one, one],
        out_specs=[one] * 2,
        compiler_params=pltpu.CompilerParams(vmem_limit_bytes=16 * MIB),
        name="drift",
    )(prm, hm, cm, h0, c0, h1, c1, idm)
    pair = pl.BlockSpec((1, 2, ny, nz), lambda i: (i, 0, 0, 0))
    de = pl.pallas_call(
        drift_edges_kernel,
        grid=(2,),
        out_shape=f32(2, 2, ny, nz),
        in_specs=[SMEM, pair, edge_rows, edge_rows, pair, one],
        out_specs=pair,
        compiler_params=pltpu.CompilerParams(vmem_limit_bytes=16 * MIB),
        name="drift_edges",
    )(prm, edge, h0, c0, e1, ide)

    vm = jnp.stack([hm[1:-1], cm[1:-1]])
    vn = jnp.stack([jnp.stack([x[0], x[-1]]) for x in (hm, cm)])
    vo = edge
    for n in range(1, slices):
        own = (slot == n).astype(jnp.int32).reshape(1)
        am = move(vm, (n - 1,), 1, 0)
        an = move(vn, (n - 1,), 1, 0)
        ao = move(vo, (n - 1,), 1, 0)
        low, high = halos(tl0, tl7, (n - 1,), 1)
        vm = call(
            coarse_mid_kernel,
            [f32(2, mid, ny, nz)],
            (own, prm, am, an, dhm, dcm, idm, vm),
            2,
            (rows - 2) * row,
            pad(mid + 2),
            40,
            "coarse_mid",
        )[0]
        vn, part = call(
            coarse_rim_kernel,
            [f32(2, 2, ny, nz)] * 2,
            (own, prm, ao, an, am, dhm, dcm, de, idm, ide, vn),
            2,
            6 * row,
            pad(6),
            40,
            "coarse_rim",
        )
        if n < slices - 1:
            vo, tl0, tl7 = call(
                coarse_edges_kernel,
                [f32(2, 2, ny, nz)] + [f32(2, ny, nz)] * 2,
                (own, prm, part, low, high, ide, vo),
                2,
                2 * row,
                limit=16,
                name="coarse_edges",
            )

    oh, oc = call(spread_kernel, [f32(1, rows, ny, nz)] * 2, (vm, vn), 0, rows * row, limit=20, name="spread")
    out_edge = pl.BlockSpec((1, 1, ny, nz), lambda i: (0, (rows - 1) * i, 0, 0))
    anyspec = pl.BlockSpec(memory_space=pl.ANY)
    return tuple(
        pl.pallas_call(
            last_edges_kernel,
            grid=(2,),
            out_shape=[f32(1, rows, ny, nz)] * 2,
            in_specs=[SMEM, SMEM, pair, whole, whole, one, pair, anyspec, anyspec],
            out_specs=[out_edge] * 2,
            input_output_aliases={7: 0, 8: 1},
            compiler_params=pltpu.CompilerParams(vmem_limit_bytes=16 * MIB),
            name="last_edges",
        )(own, prm, part, low, high, ide, vo, oh, oc)
    )


def solution(mesh):
    body = functools.partial(per_device, mesh.shape["tm"], mesh.shape["space"])
    return jax.shard_map(
        body,
        mesh=mesh,
        in_specs=(
            P("tm", "space", None, None),
            P("tm", "space", None, None),
            P("space", None, None),
            P("space", None, None),
        )
        + (P(),) * 7,
        out_specs=(P("tm", "space", None, None), P("tm", "space", None, None)),
        check_vma=False,
    )
```

time: 628 us -> 248 us (0.39)
  the two profiles are of different devices: /device:TPU:6 before, /device:TPU:11 now
where the time goes in v1:
time: 248 us; the launch traced here: 246 us
  Pallas kernels  94.9 us (38%)
  waiting for transfers between devices  80.2 us (32%)
  starting transfers between devices  43.5 us (18%)
  local copies, waits for them, and re-layouts  23.5 us (9%)
  other arithmetic  2.79 us (1%)
    pallas_call x17, Pallas kernels, call(): pl.pallas_call(kernel, out_shape=outs, in_specs=[SMEM] * smem + [VMEM] *...  86.7 us
    ppermute x23, waiting for transfers between devices, move(): return lax.ppermute(x, ('tm', 'space'), pairs)  80.2 us
    ppermute x23, starting transfers between devices, move(): return lax.ppermute(x, ('tm', 'space'), pairs)  43.5 us
    unnamed x70, local copies, waits for them, and re-layouts  22.5 us
  transfers between devices with their start and end apart: 23, of which 9 were waited for; matrix products, arithmetic and copies ran while one was open for 0% of the time, Pallas kernels for 30%

profile of v1, /device:TPU:11, one launch (start us, length us, event | category | flops | bytes accessed | tf_op | source)
XLA Modules:
  0.0 246.2 jit_solution(14472206656758525244)
XLA Ops:
  9.2 3.3 %collective-permute-start = (f32[2,512,128]{2,1,0:T(8,128)S(1)}, f32[2,512,128]{2,1,0:T(8,128)S(1)}, u32[]{:S(2)}, u32[]{:S(2)}) collective-permute-start(f32[2,512,128]{2,1,0:T(8,128)S(1)} %get-tuple-element.49), channel_id=1, source_target_pairs={{0,1},{1,2},{2,3},{3,4},{4,5},{5,6},{6,7},{8,9},{9,10},{10,11},{11... | collective-permute-start | bytes 1572872 | tf_op jit(solution)/shard_map/ppermute | solution.py:448
  12.5 3.0 %collective-permute-start.1 = (f32[2,512,128]{2,1,0:T(8,128)S(1)}, f32[2,512,128]{2,1,0:T(8,128)S(1)}, u32[]{:S(2)}, u32[]{:S(2)}) collective-permute-start(f32[2,512,128]{2,1,0:T(8,128)S(1)} %get-tuple-element.50), channel_id=1, source_target_pairs={{1,0},{2,1},{3,2},{4,3},{5,4},{6,5},{7,6},{9,8},{10,9},{11,10},{12... | collective-permute-start | bytes 1572872 | tf_op jit(solution)/shard_map/ppermute | solution.py:448
  15.6 11.6 %first_step.1 = (f32[6,512,128]{2,1,0:T(8,128)S(1)}, f32[6,512,128]{2,1,0:T(8,128)S(1)}, f32[2,2,512,128]{3,2,1,0:T(8,128)S(1)}, s32[6,512,128]{2,1,0:T(8,128)S(1)}, s32[2,512,128]{2,1,0:T(8,128)S(1)}) custom-call(f32[27]{0:T(128)S(1)} %concatenate.3.prm, f32[8,512,128]{2,1,0:T(8,128)S(1)} %bitcast.14, f32[8,512,128]{2,1,0:T(8,128)S(1)} %bitcast.18, ...), custom_call_target="tpu_custom_call" | custom-call | flops 52428800 | bytes 14680172 | tf_op jit(solution)/shard_map/first_step/pallas_call | solution.py:417
  27.3 7.1 %collective-permute-done.low = f32[2,512,128]{2,1,0:T(8,128)S(1)} collective-permute-done((f32[2,512,128]{2,1,0:T(8,128)S(1)}, f32[2,512,128]{2,1,0:T(8,128)S(1)}, u32[]{:S(2)}, u32[]{:S(2)}) %collective-permute-start) | collective-permute-done | bytes 524320 | tf_op jit(solution)/shard_map/ppermute | solution.py:448
  34.3 2.9 %collective-permute-done.1.high = f32[2,512,128]{2,1,0:T(8,128)S(1)} collective-permute-done((f32[2,512,128]{2,1,0:T(8,128)S(1)}, f32[2,512,128]{2,1,0:T(8,128)S(1)}, u32[]{:S(2)}, u32[]{:S(2)}) %collective-permute-start.1) | collective-permute-done | bytes 524320 | tf_op jit(solution)/shard_map/ppermute | solution.py:448
  40.7 4.3 %collective-permute-start.3 = (f32[2,512,128]{2,1,0:T(8,128)S(1)}, f32[2,512,128]{2,1,0:T(8,128)S(1)}, u32[]{:S(2)}, u32[]{:S(2)}) collective-permute-start(f32[2,512,128]{2,1,0:T(8,128)S(1)} %get-tuple-element.58), channel_id=1, source_target_pairs={{1,0},{2,1},{3,2},{4,3},{5,4},{6,5},{7,6},{9,8},{10,9},{11,10},{12... | collective-permute-start | bytes 1572872 | tf_op jit(solution)/shard_map/ppermute | solution.py:448
  44.9 10.2 %step.3 = (f32[6,512,128]{2,1,0:T(8,128)S(1)}, f32[6,512,128]{2,1,0:T(8,128)S(1)}, f32[2,2,512,128]{3,2,1,0:T(8,128)S(1)}) custom-call(f32[27]{0:T(128)S(1)} %concatenate.3.prm, f32[6,512,128]{2,1,0:T(8,128)S(1)} %get-tuple-element.46.hm.h1, f32[6,512,128]{2,1,0:T(8,128)S(1)} %get-tuple-element.47.cm.c1, f32[2,2,512,128]{3,2,1,0:T(8,128)S(1)} %get-tuple-element.52.edge.e1, ...), custom_call_target="tpu_custom_call" | custom-call | flops 52428800 | bytes 10485868 | tf_op jit(solution)/shard_map/step/pallas_call | solution.py:417
  55.2 7.1 %collective-permute-done.2.low = f32[2,512,128]{2,1,0:T(8,128)S(1)} collective-permute-done((f32[2,512,128]{2,1,0:T(8,128)S(1)}, f32[2,512,128]{2,1,0:T(8,128)S(1)}, u32[]{:S(2)}, u32[]{:S(2)}) %collective-permute-start.2) | collective-permute-done | bytes 524320 | tf_op jit(solution)/shard_map/ppermute | solution.py:448
  62.3 4.3 %collective-permute-done.3.high = f32[2,512,128]{2,1,0:T(8,128)S(1)} collective-permute-done((f32[2,512,128]{2,1,0:T(8,128)S(1)}, f32[2,512,128]{2,1,0:T(8,128)S(1)}, u32[]{:S(2)}, u32[]{:S(2)}) %collective-permute-start.3) | collective-permute-done | bytes 524320 | tf_op jit(solution)/shard_map/ppermute | solution.py:448
  70.0 4.3 %collective-permute-start.5 = (f32[2,512,128]{2,1,0:T(8,128)S(1)}, f32[2,512,128]{2,1,0:T(8,128)S(1)}, u32[]{:S(2)}, u32[]{:S(2)}) collective-permute-start(f32[2,512,128]{2,1,0:T(8,128)S(1)} %get-tuple-element.64), channel_id=1, source_target_pairs={{1,0},{2,1},{3,2},{4,3},{5,4},{6,5},{7,6},{9,8},{10,9},{11,10},{12... | collective-permute-start | bytes 1572872 | tf_op jit(solution)/shard_map/ppermute | solution.py:448
  74.3 10.2 %step.4 = (f32[6,512,128]{2,1,0:T(8,128)S(1)}, f32[6,512,128]{2,1,0:T(8,128)S(1)}, f32[2,2,512,128]{3,2,1,0:T(8,128)S(1)}) custom-call(f32[27]{0:T(128)S(1)} %concatenate.3.prm, f32[6,512,128]{2,1,0:T(8,128)S(1)} %get-tuple-element.54.hm, f32[6,512,128]{2,1,0:T(8,128)S(1)} %get-tuple-element.55.cm, f32[2,2,512,128]{3,2,1,0:T(8,128)S(1)} %get-tuple-element.59.edge, ...), custom_call_target="tpu_custom_call" | custom-call | flops 52428800 | bytes 10485868 | tf_op jit(solution)/shard_map/step/pallas_call | solution.py:417
  84.5 7.8 %collective-permute-done.4.low = f32[2,512,128]{2,1,0:T(8,128)S(1)} collective-permute-done((f32[2,512,128]{2,1,0:T(8,128)S(1)}, f32[2,512,128]{2,1,0:T(8,128)S(1)}, u32[]{:S(2)}, u32[]{:S(2)}) %collective-permute-start.4) | collective-permute-done | bytes 524320 | tf_op jit(solution)/shard_map/ppermute | solution.py:448
  92.4 3.6 %collective-permute-done.5.high = f32[2,512,128]{2,1,0:T(8,128)S(1)} collective-permute-done((f32[2,512,128]{2,1,0:T(8,128)S(1)}, f32[2,512,128]{2,1,0:T(8,128)S(1)}, u32[]{:S(2)}, u32[]{:S(2)}) %collective-permute-start.5) | collective-permute-done | bytes 524320 | tf_op jit(solution)/shard_map/ppermute | solution.py:448
  96.0 2.4 edges.6
  98.4 10.2 %step.5 = (f32[6,512,128]{2,1,0:T(8,128)S(1)}, f32[6,512,128]{2,1,0:T(8,128)S(1)}, f32[2,2,512,128]{3,2,1,0:T(8,128)S(1)}) custom-call(f32[27]{0:T(128)S(1)} %concatenate.3.prm, f32[6,512,128]{2,1,0:T(8,128)S(1)} %get-tuple-element.60.hm, f32[6,512,128]{2,1,0:T(8,128)S(1)} %get-tuple-element.61.cm, f32[2,2,512,128]{3,2,1,0:T(8,128)S(1)} %get-tuple-element.65.edge, ...), custom_call_target="tpu_custom_call" | custom-call | flops 52428800 | bytes 10485868 | tf_op jit(solution)/shard_map/step/pallas_call | solution.py:417
  111.3 2.0 collective-permute-start.10
  117.2 4.3 %collective-permute-start.7 = (f32[2,512,128]{2,1,0:T(8,128)}, f32[2,512,128]{2,1,0:T(8,128)}, u32[]{:S(2)}, u32[]{:S(2)}) collective-permute-start(f32[2,512,128]{2,1,0:T(8,128)} %get-tuple-element.68), channel_id=1, source_target_pairs={{1,0},{2,1},{3,2},{4,3},{5,4},{6,5},{7,6},{9,8},{10,9},{11,10},{12... | collective-permute-start | bytes 1572872 | tf_op jit(solution)/shard_map/ppermute | solution.py:448
  130.3 2.6 %drift.1 = (f32[6,512,128]{2,1,0:T(8,128)S(1)}, f32[6,512,128]{2,1,0:T(8,128)S(1)}) custom-call(f32[27]{0:T(128)S(1)} %concatenate.3.prm, f32[6,512,128]{2,1,0:T(8,128)S(1)} %copy-done.22, f32[6,512,128]{2,1,0:T(8,128)S(1)} %copy-done.24, f32[8,512,128]{2,1,0:T(8,128)S(1)} %bitcast.15, f32[8,512,128]{2,1,0:T(8,128)S(1)} %bitcast.19, ...), custom_call_target="tpu_custom_call" | custom-call | tf_op jit(solution)/shard_map/drift/pallas_call | solution.py:506
  133.0 6.9 %collective-permute-done.6.low = f32[2,512,128]{2,1,0:T(8,128)} collective-permute-done((f32[2,512,128]{2,1,0:T(8,128)}, f32[2,512,128]{2,1,0:T(8,128)}, u32[]{:S(2)}, u32[]{:S(2)}) %collective-permute-start.6) | collective-permute-done | bytes 524320 | tf_op jit(solution)/shard_map/ppermute | solution.py:448
  139.9 3.6 %collective-permute-done.7.high = f32[2,512,128]{2,1,0:T(8,128)} collective-permute-done((f32[2,512,128]{2,1,0:T(8,128)}, f32[2,512,128]{2,1,0:T(8,128)}, u32[]{:S(2)}, u32[]{:S(2)}) %collective-permute-start.7) | collective-permute-done | bytes 524320 | tf_op jit(solution)/shard_map/ppermute | solution.py:448
  143.5 3.1 %edges.7 = (f32[2,2,512,128]{3,2,1,0:T(8,128)S(1)}, f32[2,512,128]{2,1,0:T(8,128)}, f32[2,512,128]{2,1,0:T(8,128)}) custom-call(f32[27]{0:T(128)S(1)} %concatenate.3.prm, f32[2,2,512,128]{3,2,1,0:T(8,128)S(1)} %copy-done.32, f32[2,512,128]{2,1,0:T(8,128)} %collective-permute-done.6.low, f32[2,512,128]{2,1,0:T(8,128)} %collective-permute-done.7.high, ...), custom_call_target="tpu_custom_call" | custom-call | flops 13107200 | bytes 4718700 | tf_op jit(solution)/shard_map/edges/pallas_call | solution.py:417
  147.4 4.1 %coarse_mid.3.old = f32[2,4,512,128]{3,2,1,0:T(8,128)} custom-call(s32[1]{0:T(128)} %bitcast.2.own, f32[27]{0:T(128)S(1)} %concatenate.3.prm, f32[2,4,512,128]{3,2,1,0:T(8,128)} %collective-permute-done.10.vm, f32[2,2,512,128]{3,2,1,0:T(8,128)S(1)} %collective-permute-done.9.vn, f32[6,512,128]{2,1,0:T(8,128)S(1)} %get-tuple-element.72.dhm, ...), custom_call_target="tpu_custom_call" | custom-call | flops 39321600 | bytes 12058736 | tf_op jit(solution)/shard_map/coarse_mid/pallas_call | solution.py:417
  151.5 2.0 collective-permute-start.15
  154.9 3.0 %coarse_rim.3 = (f32[2,2,512,128]{3,2,1,0:T(8,128)}, f32[2,2,512,128]{3,2,1,0:T(8,128)S(1)}) custom-call(s32[1]{0:T(128)} %bitcast.2.own, f32[27]{0:T(128)S(1)} %concatenate.3.prm, f32[2,2,512,128]{3,2,1,0:T(8,128)S(1)} %collective-permute-done.8.vo, f32[2,2,512,128]{3,2,1,0:T(8,128)S(1)} %copy-done.28, f32[2,4,512,128]{3,2,1,0:T(8,128)} %collective-permute-done.10.vm, ...), custom_call_target="tpu_custom_call" | custom-call | flops 39321600 | bytes 13631600 | tf_op jit(solution)/shard_map/coarse_rim/pallas_call | solution.py:417
  168.1 4.0 %coarse_mid.4.old = f32[2,4,512,128]{3,2,1,0:T(8,128)} custom-call(s32[1]{0:T(128)} %bitcast.1.own, f32[27]{0:T(128)S(1)} %concatenate.3.prm, f32[2,4,512,128]{3,2,1,0:T(8,128)} %collective-permute-done.15.vm, f32[2,2,512,128]{3,2,1,0:T(8,128)} %collective-permute-done.14.vn, f32[6,512,128]{2,1,0:T(8,128)S(1)} %copy-done.1, f32[6,512,128]{2,1,0:T(8,128)S(1)} %copy-done.4, ...), custom_call_target="tpu_custom_call" | custom-call | flops 39321600 | bytes 12058736 | tf_op jit(solution)/shard_map/coarse_mid/pallas_call | solution.py:417
  174.9 3.2 %coarse_rim.4 = (f32[2,2,512,128]{3,2,1,0:T(8,128)}, f32[2,2,512,128]{3,2,1,0:T(8,128)S(1)}) custom-call(s32[1]{0:T(128)} %bitcast.1.own, f32[27]{0:T(128)S(1)} %concatenate.3.prm, f32[2,2,512,128]{3,2,1,0:T(8,128)S(1)} %collective-permute-done.13.vo, f32[2,2,512,128]{3,2,1,0:T(8,128)} %collective-permute-done.14.vn, ...), custom_call_target="tpu_custom_call" | custom-call | flops 39321600 | bytes 13631600 | tf_op jit(solution)/shard_map/coarse_rim/pallas_call | solution.py:417
  179.4 2.0 coarse_edges.3
  185.3 36.8 %collective-permute-done.19.vn = f32[2,2,512,128]{3,2,1,0:T(8,128)} collective-permute-done((f32[2,2,512,128]{3,2,1,0:T(8,128)}, f32[2,2,512,128]{3,2,1,0:T(8,128)}, u32[]{:S(2)}, u32[]{:S(2)}) %collective-permute-start.19) | collective-permute-done | bytes 1048608 | tf_op jit(solution)/shard_map/ppermute | solution.py:448
  224.9 8.0 %coarse_mid.5.vm = f32[2,4,512,128]{3,2,1,0:T(8,128)S(1)} custom-call(s32[1]{0:T(128)} %bitcast.own, f32[27]{0:T(128)S(1)} %concatenate.3.prm, f32[2,4,512,128]{3,2,1,0:T(8,128)} %collective-permute-done.20.vm, f32[2,2,512,128]{3,2,1,0:T(8,128)} %collective-permute-done.19.vn, f32[6,512,128]{2,1,0:T(8,128)S(1)} %copy-done.2, f32[6,512,128]{2,1,0:T(8,128)S(1)} %copy-done.5, ...), custom_call_target="tpu_custom_call" | custom-call | flops 39321600 | bytes 12058736 | tf_op jit(solution)/shard_map/coarse_mid/pallas_call | solution.py:417
  233.0 8.1 %coarse_rim.5 = (f32[2,2,512,128]{3,2,1,0:T(8,128)S(1)}, f32[2,2,512,128]{3,2,1,0:T(8,128)S(1)}) custom-call(s32[1]{0:T(128)} %bitcast.own, f32[27]{0:T(128)S(1)} %concatenate.3.prm, f32[2,2,512,128]{3,2,1,0:T(8,128)} %collective-permute-done.18.vo, f32[2,2,512,128]{3,2,1,0:T(8,128)} %collective-permute-done.19.vn, ...), custom_call_target="tpu_custom_call" | custom-call | flops 39321600 | bytes 13631600 | tf_op jit(solution)/shard_map/coarse_rim/pallas_call | solution.py:417
  241.1 2.2 spread.1
  243.3 2.9 %last_edges.1 = (f32[1,8,512,128]{3,2,1,0:T(8,128)}, f32[1,8,512,128]{3,2,1,0:T(8,128)}) custom-call(s32[1]{0:T(128)} %bitcast.own, f32[27]{0:T(128)S(1)} %concatenate.3.prm, f32[2,2,512,128]{3,2,1,0:T(8,128)S(1)} %get-tuple-element.84.part, f32[2,512,128]{2,1,0:T(8,128)} %collective-permute-done.21.low, ...), custom_call_target="tpu_custom_call", output_to_operand_aliasing={{0}: (7, {}), {1}: (8, {})} | custom-call | tf_op jit(solution)/shard_map/last_edges/pallas_call | solution.py:570
  (112 shorter events, 53.6 us)
Async XLA Ops:
  7.8 7.7 %copy-start.7 = (f32[1,8,512,128]{3,2,1,0:T(8,128)S(1)}, f32[1,8,512,128]{3,2,1,0:T(8,128)}, u32[]{:S(2)}) copy-start(f32[1,8,512,128]{3,2,1,0:T(8,128)} %param.11) | copy-start | bytes 6291460
  7.8 7.7 %copy-start.11 = (f32[1,8,512,128]{3,2,1,0:T(8,128)S(1)}, f32[1,8,512,128]{3,2,1,0:T(8,128)}, u32[]{:S(2)}) copy-start(f32[1,8,512,128]{3,2,1,0:T(8,128)} %param.12) | copy-start | bytes 6291460
  7.8 7.8 %copy-start.15 = (s32[8,512,128]{2,1,0:T(8,128)S(1)}, s32[8,512,128]{2,1,0:T(8,128)}, u32[]{:S(2)}) copy-start(s32[8,512,128]{2,1,0:T(8,128)} %mat.3) | copy-start | bytes 6291460
  9.2 25.1 %collective-permute-start = (f32[2,512,128]{2,1,0:T(8,128)S(1)}, f32[2,512,128]{2,1,0:T(8,128)S(1)}, u32[]{:S(2)}, u32[]{:S(2)}) collective-permute-start(f32[2,512,128]{2,1,0:T(8,128)S(1)} %get-tuple-element.49), channel_id=1, source_target_pairs={{0,1},{1,2},{2,3},{3,4},{4,5},{5,6},{6,7},{8,9},{9,10},{10,11},{11... | collective-permute-start | bytes 1572872 | tf_op jit(solution)/shard_map/ppermute | solution.py:448
  12.5 24.7 %collective-permute-start.1 = (f32[2,512,128]{2,1,0:T(8,128)S(1)}, f32[2,512,128]{2,1,0:T(8,128)S(1)}, u32[]{:S(2)}, u32[]{:S(2)}) collective-permute-start(f32[2,512,128]{2,1,0:T(8,128)S(1)} %get-tuple-element.50), channel_id=1, source_target_pairs={{1,0},{2,1},{3,2},{4,3},{5,4},{6,5},{7,6},{9,8},{10,9},{11,10},{12... | collective-permute-start | bytes 1572872 | tf_op jit(solution)/shard_map/ppermute | solution.py:448
  27.2 27.9 %copy-start.17 = (f32[6,512,128]{2,1,0:T(8,128)}, f32[6,512,128]{2,1,0:T(8,128)S(1)}, u32[]{:S(2)}) copy-start(f32[6,512,128]{2,1,0:T(8,128)S(1)} %get-tuple-element.46.hm.h1) | copy-start | bytes 4718596
  27.2 27.9 %copy-start.19 = (f32[6,512,128]{2,1,0:T(8,128)}, f32[6,512,128]{2,1,0:T(8,128)S(1)}, u32[]{:S(2)}) copy-start(f32[6,512,128]{2,1,0:T(8,128)S(1)} %get-tuple-element.47.cm.c1) | copy-start | bytes 4718596
  38.7 16.5 %copy-start.25 = (f32[2,2,512,128]{3,2,1,0:T(8,128)}, f32[2,2,512,128]{3,2,1,0:T(8,128)S(1)}, u32[]{:S(2)}) copy-start(f32[2,2,512,128]{3,2,1,0:T(8,128)S(1)} %get-tuple-element.52.edge.e1) | copy-start | bytes 3145732
  38.7 23.6 %collective-permute-start.2 = (f32[2,512,128]{2,1,0:T(8,128)S(1)}, f32[2,512,128]{2,1,0:T(8,128)S(1)}, u32[]{:S(2)}, u32[]{:S(2)}) collective-permute-start(f32[2,512,128]{2,1,0:T(8,128)S(1)} %get-tuple-element.57), channel_id=1, source_target_pairs={{0,1},{1,2},{2,3},{3,4},{4,5},{5,6},{6,7},{8,9},{9,10},{10,11},{11... | collective-permute-start | bytes 1572872 | tf_op jit(solution)/shard_map/ppermute | solution.py:448
  40.7 26.0 %collective-permute-start.3 = (f32[2,512,128]{2,1,0:T(8,128)S(1)}, f32[2,512,128]{2,1,0:T(8,128)S(1)}, u32[]{:S(2)}, u32[]{:S(2)}) collective-permute-start(f32[2,512,128]{2,1,0:T(8,128)S(1)} %get-tuple-element.58), channel_id=1, source_target_pairs={{1,0},{2,1},{3,2},{4,3},{5,4},{6,5},{7,6},{9,8},{10,9},{11,10},{12... | collective-permute-start | bytes 1572872 | tf_op jit(solution)/shard_map/ppermute | solution.py:448
  68.1 24.3 %collective-permute-start.4 = (f32[2,512,128]{2,1,0:T(8,128)S(1)}, f32[2,512,128]{2,1,0:T(8,128)S(1)}, u32[]{:S(2)}, u32[]{:S(2)}) collective-permute-start(f32[2,512,128]{2,1,0:T(8,128)S(1)} %get-tuple-element.63), channel_id=1, source_target_pairs={{0,1},{1,2},{2,3},{3,4},{4,5},{5,6},{6,7},{8,9},{9,10},{10,11},{11... | collective-permute-start | bytes 1572872 | tf_op jit(solution)/shard_map/ppermute | solution.py:448
  70.0 26.0 %collective-permute-start.5 = (f32[2,512,128]{2,1,0:T(8,128)S(1)}, f32[2,512,128]{2,1,0:T(8,128)S(1)}, u32[]{:S(2)}, u32[]{:S(2)}) collective-permute-start(f32[2,512,128]{2,1,0:T(8,128)S(1)} %get-tuple-element.64), channel_id=1, source_target_pairs={{1,0},{2,1},{3,2},{4,3},{5,4},{6,5},{7,6},{9,8},{10,9},{11,10},{12... | collective-permute-start | bytes 1572872 | tf_op jit(solution)/shard_map/ppermute | solution.py:448
  111.3 36.1 %collective-permute-start.10 = (f32[2,4,512,128]{3,2,1,0:T(8,128)}, f32[2,4,512,128]{3,2,1,0:T(8,128)}, u32[]{:S(2)}, u32[]{:S(2)}) collective-permute-start(f32[2,4,512,128]{3,2,1,0:T(8,128)} %pad_maximum_fusion.old), channel_id=1, source_target_pairs={{0,8},{1,9},{2,10},{3,11},{4,12},{5,13},{6,14},{7,15}} | collective-permute-start | bytes 6291464 | tf_op jit(solution)/shard_map/ppermute | solution.py:448
  114.6 32.8 %collective-permute-start.9 = (f32[2,2,512,128]{3,2,1,0:T(8,128)}, f32[2,2,512,128]{3,2,1,0:T(8,128)S(1)}, u32[]{:S(2)}, u32[]{:S(2)}) collective-permute-start(f32[2,2,512,128]{3,2,1,0:T(8,128)} %pad_maximum_fusion.1.old), channel_id=1, source_target_pairs={{0,8},{1,9},{2,10},{3,11},{4,12},{5,13},{6,14},{7,15}} | collective-permute-start | bytes 3145736 | tf_op jit(solution)/shard_map/ppermute | solution.py:448
  115.3 24.6 %collective-permute-start.6 = (f32[2,512,128]{2,1,0:T(8,128)}, f32[2,512,128]{2,1,0:T(8,128)}, u32[]{:S(2)}, u32[]{:S(2)}) collective-permute-start(f32[2,512,128]{2,1,0:T(8,128)} %get-tuple-element.67), channel_id=1, source_target_pairs={{0,1},{1,2},{2,3},{3,4},{4,5},{5,6},{6,7},{8,9},{9,10},{10,11},{11... | collective-permute-start | bytes 1572872 | tf_op jit(solution)/shard_map/ppermute | solution.py:448
  117.2 26.3 %collective-permute-start.7 = (f32[2,512,128]{2,1,0:T(8,128)}, f32[2,512,128]{2,1,0:T(8,128)}, u32[]{:S(2)}, u32[]{:S(2)}) collective-permute-start(f32[2,512,128]{2,1,0:T(8,128)} %get-tuple-element.68), channel_id=1, source_target_pairs={{1,0},{2,1},{3,2},{4,3},{5,4},{6,5},{7,6},{9,8},{10,9},{11,10},{12... | collective-permute-start | bytes 1572872 | tf_op jit(solution)/shard_map/ppermute | solution.py:448
  130.3 13.2 %copy-start.32 = (f32[2,2,512,128]{3,2,1,0:T(8,128)S(1)}, f32[2,2,512,128]{3,2,1,0:T(8,128)}, u32[]{:S(2)}) copy-start(f32[2,2,512,128]{3,2,1,0:T(8,128)} %copy-done.31) | copy-start | bytes 3145732
  133.0 21.9 %copy-start = (f32[6,512,128]{2,1,0:T(8,128)}, f32[6,512,128]{2,1,0:T(8,128)S(1)}, u32[]{:S(2)}) copy-start(f32[6,512,128]{2,1,0:T(8,128)S(1)} %get-tuple-element.72.dhm) | copy-start | bytes 4718596
  133.0 21.9 %copy-start.3 = (f32[6,512,128]{2,1,0:T(8,128)}, f32[6,512,128]{2,1,0:T(8,128)S(1)}, u32[]{:S(2)}) copy-start(f32[6,512,128]{2,1,0:T(8,128)S(1)} %get-tuple-element.73.dcm) | copy-start | bytes 4718596
  146.6 8.2 %collective-permute-start.8 = (f32[2,2,512,128]{3,2,1,0:T(8,128)S(1)}, f32[2,2,512,128]{3,2,1,0:T(8,128)S(1)}, u32[]{:S(2)}, u32[]{:S(2)}) collective-permute-start(f32[2,2,512,128]{3,2,1,0:T(8,128)S(1)} %get-tuple-element.69.e4.old), channel_id=1, source_target_pairs={{0,8},{1,9},{2,10},{3,11},{4,12},{5,13},{6,14},{7,15}} | collective-permute-start | bytes 3145736 | tf_op jit(solution)/shard_map/ppermute | solution.py:448
  151.5 16.6 %collective-permute-start.15 = (f32[2,4,512,128]{3,2,1,0:T(8,128)}, f32[2,4,512,128]{3,2,1,0:T(8,128)}, u32[]{:S(2)}, u32[]{:S(2)}) collective-permute-start(f32[2,4,512,128]{3,2,1,0:T(8,128)} %coarse_mid.3.old), channel_id=1, source_target_pairs={{8,16},{9,17},{10,18},{11,19},{12,20},{13,21},{14,22},{15,23}} | collective-permute-start | bytes 6291464 | tf_op jit(solution)/shard_map/ppermute | solution.py:448
  158.8 9.3 %collective-permute-start.14 = (f32[2,2,512,128]{3,2,1,0:T(8,128)}, f32[2,2,512,128]{3,2,1,0:T(8,128)}, u32[]{:S(2)}, u32[]{:S(2)}) collective-permute-start(f32[2,2,512,128]{3,2,1,0:T(8,128)} %get-tuple-element.78.old), channel_id=1, source_target_pairs={{8,16},{9,17},{10,18},{11,19},{12,20},{13,21},{14,22},{15,23}} | collective-permute-start | bytes 3145736 | tf_op jit(solution)/shard_map/ppermute | solution.py:448
  160.5 3.0 %collective-permute-start.11 = (f32[2,512,128]{2,1,0:T(8,128)}, f32[2,512,128]{2,1,0:T(8,128)}, u32[]{:S(2)}, u32[]{:S(2)}) collective-permute-start(f32[2,512,128]{2,1,0:T(8,128)} %get-tuple-element.75), channel_id=1, source_target_pairs={{0,9},{1,10},{2,11},{3,12},{4,13},{5,14},{6,15}} | collective-permute-start | bytes 1572872 | tf_op jit(solution)/shard_map/ppermute | solution.py:448
  161.9 1.5 collective-permute-start.12
  167.3 7.5 %collective-permute-start.13 = (f32[2,2,512,128]{3,2,1,0:T(8,128)S(1)}, f32[2,2,512,128]{3,2,1,0:T(8,128)S(1)}, u32[]{:S(2)}, u32[]{:S(2)}) collective-permute-start(f32[2,2,512,128]{3,2,1,0:T(8,128)S(1)} %get-tuple-element.77.old), channel_id=1, source_target_pairs={{8,16},{9,17},{10,18},{11,19},{12,20},{13,21},{14,22},{15,23}} | collective-permute-start | bytes 3145736 | tf_op jit(solution)/shard_map/ppermute | solution.py:448
  172.1 49.9 %collective-permute-start.20 = (f32[2,4,512,128]{3,2,1,0:T(8,128)}, f32[2,4,512,128]{3,2,1,0:T(8,128)}, u32[]{:S(2)}, u32[]{:S(2)}) collective-permute-start(f32[2,4,512,128]{3,2,1,0:T(8,128)} %coarse_mid.4.old), channel_id=1, source_target_pairs={{16,24},{17,25},{18,26},{19,27},{20,28},{21,29},{22,30},{23,31}} | collective-permute-start | bytes 6291464 | tf_op jit(solution)/shard_map/ppermute | solution.py:448
  173.4 6.0 %collective-permute-start.16 = (f32[2,512,128]{2,1,0:T(8,128)S(1)}, f32[2,512,128]{2,1,0:T(8,128)S(1)}, u32[]{:S(2)}, u32[]{:S(2)}) collective-permute-start(f32[2,512,128]{2,1,0:T(8,128)S(1)} %get-tuple-element.80), channel_id=1, source_target_pairs={{8,17},{9,18},{10,19},{11,20},{12,21},{13,22},{14,23}} | collective-permute-start | bytes 1572872 | tf_op jit(solution)/shard_map/ppermute | solution.py:448
  174.1 5.3 %collective-permute-start.17 = (f32[2,512,128]{2,1,0:T(8,128)S(1)}, f32[2,512,128]{2,1,0:T(8,128)S(1)}, u32[]{:S(2)}, u32[]{:S(2)}) collective-permute-start(f32[2,512,128]{2,1,0:T(8,128)S(1)} %get-tuple-element.81), channel_id=1, source_target_pairs={{9,16},{10,17},{11,18},{12,19},{13,20},{14,21},{15,22}} | collective-permute-start | bytes 1572872 | tf_op jit(solution)/shard_map/ppermute | solution.py:448
  178.1 44.0 %collective-permute-start.19 = (f32[2,2,512,128]{3,2,1,0:T(8,128)}, f32[2,2,512,128]{3,2,1,0:T(8,128)}, u32[]{:S(2)}, u32[]{:S(2)}) collective-permute-start(f32[2,2,512,128]{3,2,1,0:T(8,128)} %get-tuple-element.83.old), channel_id=1, source_target_pairs={{16,24},{17,25},{18,26},{19,27},{20,28},{21,29},{22,30},{23,31}} | collective-permute-start | bytes 3145736 | tf_op jit(solution)/shard_map/ppermute | solution.py:448
  181.4 51.6 %collective-permute-start.18 = (f32[2,2,512,128]{3,2,1,0:T(8,128)}, f32[2,2,512,128]{3,2,1,0:T(8,128)}, u32[]{:S(2)}, u32[]{:S(2)}) collective-permute-start(f32[2,2,512,128]{3,2,1,0:T(8,128)} %get-tuple-element.82.old), channel_id=1, source_target_pairs={{16,24},{17,25},{18,26},{19,27},{20,28},{21,29},{22,30},{23,31}} | collective-permute-start | bytes 3145736 | tf_op jit(solution)/shard_map/ppermute | solution.py:448
  182.7 60.6 %collective-permute-start.21 = (f32[2,512,128]{2,1,0:T(8,128)}, f32[2,512,128]{2,1,0:T(8,128)}, u32[]{:S(2)}, u32[]{:S(2)}) collective-permute-start(f32[2,512,128]{2,1,0:T(8,128)} %get-tuple-element.85), channel_id=1, source_target_pairs={{16,25},{17,26},{18,27},{19,28},{20,29},{21,30},{22,31}} | collective-permute-start | bytes 1572872 | tf_op jit(solution)/shard_map/ppermute | solution.py:448
  184.0 59.3 %collective-permute-start.22 = (f32[2,512,128]{2,1,0:T(8,128)}, f32[2,512,128]{2,1,0:T(8,128)}, u32[]{:S(2)}, u32[]{:S(2)}) collective-permute-start(f32[2,512,128]{2,1,0:T(8,128)} %get-tuple-element.86), channel_id=1, source_target_pairs={{17,24},{18,25},{19,26},{20,27},{21,28},{22,29},{23,30}} | collective-permute-start | bytes 1572872 | tf_op jit(solution)/shard_map/ppermute | solution.py:448
  (26 other events, 72.3 us)
